TPU v7x, 512 devices: a whole 4x4x16 slice. The times are simulated.
512 devices in a mesh: blk: 64 (over z, y_hi, core), dim: 8 (over y_lo, x).
Axes of the slice: x: 4, y: 4 (y_hi: 2, y_lo: 2; y = y_hi * 2 + y_lo), z: 16, core: 2. Of those that a mesh axis runs over, the one named last changes fastest.
Arguments:
- queries: bfloat16 [12288, 4096], P('blk', 'dim')
- passages: bfloat16 [12288, 4096], P('blk', 'dim')
- negatives: bfloat16 [24576, 4096], P('blk', 'dim')
- hard_index: int32 [12288, 7], P('blk'), may hold values from 0 to 24575, as said below
Outputs:
- grad_queries: float32 [12288, 4096], P('blk', 'dim')
- document_derivative: float32 [12288, 4096], P('blk', 'dim')
- grad_negatives: float32 [24576, 4096], P('blk', 'dim')
Inputs may be any that keep to these rules, and one draw needn't show every extreme that they name: `hard_index`: pool rows are owned in blocks of 384: row r belongs to block r // 384. The 1344 entries of one block of queries name at most 42 rows of any one owning block, and exactly 42 rows of one owning block that is the same for every block of queries; entries may repeat.
All inputs are finite; a program needn't handle non-finite values.
Results may differ from a plain program's by a relative error of at most 0.012.
Values may be sent and summed in bfloat16 or wider, within the bound.
A program may use at most 128 MiB of HBM per device.

v0:
```python
import jax
import jax.numpy as jnp
from jax import lax
from jax.sharding import PartitionSpec as P

WINDOW = 16
HARD = 7


logit_divisor = 0.02


def shifted(value, axis, steps):
    count = lax.axis_size(axis)
    pairs = [(source, (source + steps) % count) for source in range(count)]
    return lax.ppermute(value, axis, pairs)


def transposed_product(weight_tile, rows_in):
    return lax.dot_general(
        weight_tile, rows_in, (((0,), (0,)), ((), ())), preferred_element_type=jnp.float32
    )


def on_device(queries, passages, negatives, hard_index):
    rows_dev, feature_width = queries.shape
    neg_rows = negatives.shape[0]
    blocks = lax.axis_size("blk")
    capacity = 2 * HARD * rows_dev // blocks
    flat_ids = hard_index.reshape(-1)
    owner_of = flat_ids // neg_rows
    local_row = flat_ids % neg_rows
    onehot = (owner_of[:, None] == jnp.arange(blocks, dtype=jnp.int32)[None, :]).astype(jnp.int32)
    before = jnp.cumsum(onehot, axis=0) - onehot
    rank_in = jnp.sum(before * onehot, axis=1)
    slot_of = owner_of * capacity + rank_in
    wanted = (
        jnp.zeros((blocks * capacity,), jnp.int32)
        .at[slot_of]
        .set(local_row)
        .reshape(blocks, capacity)
    )
    asked_rows = lax.all_to_all(wanted, "blk", split_axis=0, concat_axis=0, tiled=True)
    found_rows = negatives[asked_rows]
    returned = lax.all_to_all(found_rows, "blk", split_axis=0, concat_axis=0, tiled=True)
    mined_foil_vectors = returned.reshape(blocks * capacity, feature_width)[slot_of].reshape(
        rows_dev, HARD, feature_width
    )
    hard_part = jnp.einsum(
        "eo,ezo->ez", queries, mined_foil_vectors, preferred_element_type=jnp.float32
    )

    def cycle_step(current):
        return shifted(current, "blk", -1)

    own_tile = jnp.dot(queries, passages.T, preferred_element_type=jnp.float32)
    first_tile, mined_foil_logits = lax.psum((own_tile, hard_part), "dim")

    def scored_step(current, unused):
        following = cycle_step(current)
        score_tile = lax.psum(
            jnp.dot(queries, following.T, preferred_element_type=jnp.float32), "dim"
        )
        return (following, (following, score_tile))

    unused_last, (later_blocks, later_tiles) = lax.scan(
        scored_step, passages, None, length=WINDOW - 1
    )
    adjacent_reach = jnp.concatenate([passages[None], later_blocks], axis=0).reshape(
        WINDOW * rows_dev, feature_width
    )
    cosine_logits = jnp.concatenate(
        [first_tile, jnp.transpose(later_tiles, (1, 0, 2)).reshape(rows_dev, -1)], axis=1
    )
    cosine_logits = cosine_logits / logit_divisor
    mined_foil_logits = mined_foil_logits / logit_divisor
    row_max = jnp.maximum(jnp.max(cosine_logits, axis=1), jnp.max(mined_foil_logits, axis=1))
    row_total = jnp.sum(jnp.exp(cosine_logits - row_max[:, None]), axis=1) + jnp.sum(
        jnp.exp(mined_foil_logits - row_max[:, None]), axis=1
    )
    log_total = row_max + jnp.log(row_total)
    probable = jnp.exp(cosine_logits - log_total[:, None])
    eye_rows = jnp.eye(rows_dev, dtype=jnp.float32)
    probable = jnp.concatenate([probable[:, :rows_dev] - eye_rows, probable[:, rows_dev:]], axis=1)
    normalized_probabilities = probable.astype(jnp.bfloat16)
    mined_foil_probabilities = jnp.exp(mined_foil_logits - log_total[:, None]).astype(jnp.bfloat16)
    grad_queries = (
        jnp.dot(normalized_probabilities, adjacent_reach, preferred_element_type=jnp.float32)
        + jnp.einsum(
            "em,emz->ez",
            mined_foil_probabilities,
            mined_foil_vectors,
            preferred_element_type=jnp.float32,
        )
    ) / logit_divisor
    relayed_vectors = (
        mined_foil_probabilities.astype(jnp.float32)[:, :, None]
        * queries.astype(jnp.float32)[:, None, :]
        / logit_divisor
    ).astype(jnp.bfloat16)
    outgoing = (
        jnp.zeros((blocks * capacity, feature_width), jnp.bfloat16)
        .at[slot_of]
        .set(relayed_vectors.reshape(-1, feature_width))
    )
    incoming = lax.all_to_all(
        outgoing.reshape(blocks, capacity, feature_width),
        "blk",
        split_axis=0,
        concat_axis=0,
        tiled=True,
    )
    grad_negatives = (
        jnp.zeros((neg_rows, feature_width), jnp.float32)
        .at[asked_rows.reshape(-1)]
        .add(incoming.reshape(-1, feature_width).astype(jnp.float32))
    )

    def carry_step(accumulated_sum_so_far, shift_count):
        column = (WINDOW - 1 - shift_count) * rows_dev
        weight_tile = lax.dynamic_slice_in_dim(normalized_probabilities, column, rows_dev, 1)
        accumulated_sum_so_far = accumulated_sum_so_far + transposed_product(weight_tile, queries)
        return (shifted(accumulated_sum_so_far, "blk", 1), None)

    start_sums = jnp.zeros((rows_dev, feature_width), jnp.float32)
    accumulated_sum_so_far, unused_out = lax.scan(
        carry_step, start_sums, jnp.arange(WINDOW - 1, dtype=jnp.int32)
    )
    accumulated_sum_so_far = accumulated_sum_so_far + transposed_product(
        normalized_probabilities[:, :rows_dev], queries
    )
    document_derivative = accumulated_sum_so_far / logit_divisor
    return (grad_queries, document_derivative, grad_negatives)


def solution(mesh):
    placed = (P("blk", "dim"), P("blk", "dim"), P("blk", "dim"), P("blk", None))
    return jax.shard_map(
        on_device,
        mesh=mesh,
        in_specs=placed,
        out_specs=(P("blk", "dim"), P("blk", "dim"), P("blk", "dim")),
        check_vma=False,
    )
```

profile of v0, /device:TPU:1, one launch (start us, length us, event | category | flops | bytes accessed | tf_op | source)
XLA Modules:
  0.0 2239.0 jit_solution(8016346535510576051)
XLA Ops:
  10.9 18.1 reduce-window.6
  30.5 7.6 scatter_custom_fusion
  38.3 34.3 %all_to_all.22 = s32[64,1,42]{2,1,0:T(1,128)S(1)} all-to-all(s32[64,1,42]{2,1,0:T(1,128)S(1)} %bitcast.58), channel_id=1, replica_groups=mesh['blk'=64,'dim'=8] {'blk'}, dimensions={0} | all-to-all | bytes 21504 | tf_op jit(solution)/shard_map/all_to_all | solution.py:43
  72.8 8.6 gather_fusion
  83.9 5.7 all-to-all-start.1
  90.5 1590.3 %while.24 = (s32[]{:T(128)}, bf16[192,512]{1,0:T(8,128)(2,1)S(1)}, bf16[15,192,512]{2,1,0:T(8,128)(2,1)}, f32[15,192,192]{2,1,0:T(8,128)}, bf16[192,512]{1,0:T(8,128)(2,1)S(1)}, /*index=5*/s32[]{:T(128)}) while((s32[]{:T(128)}, bf16[192,512]{1,0:T(8,128)(2,1)S(1)}, bf16[15,192,512]{2,1,0:T(8,128)(2,1)}, f32[15,192,192]{2,1,0:T(8,128)}, ...), condition=%wide.region_3.4_spmd, body=%wide.region_1.3_spmd.sunk | while | flops 37785600 | bytes 3489957 | solution.py:66
  93.1 8.1 collective-permute-done
  102.9 210.3 %all-reduce.6.cloned.1.call-done = f32[1,192,192]{2,1,0:T(8,128)} async-done(((f32[1,192,192]{2,1,0:T(8,128)}), f32[1,192,192]{2,1,0:T(8,128)}) %all-reduce.6.cloned.1.call-update) | async-done | bytes 147472 | tf_op jit(solution)/shard_map/while/body/eval_jaxpr/psum | solution.py:61
  314.8 7.5 collective-permute-start
  322.3 5.7 collective-permute-done
  329.6 81.2 %all-reduce.6.cloned.1.call-done = f32[1,192,192]{2,1,0:T(8,128)} async-done(((f32[1,192,192]{2,1,0:T(8,128)}), f32[1,192,192]{2,1,0:T(8,128)}) %all-reduce.6.cloned.1.call-update) | async-done | bytes 147472 | tf_op jit(solution)/shard_map/while/body/eval_jaxpr/psum | solution.py:61
  412.4 7.5 collective-permute-start
  427.1 81.2 %all-reduce.6.cloned.1.call-done = f32[1,192,192]{2,1,0:T(8,128)} async-done(((f32[1,192,192]{2,1,0:T(8,128)}), f32[1,192,192]{2,1,0:T(8,128)}) %all-reduce.6.cloned.1.call-update) | async-done | bytes 147472 | tf_op jit(solution)/shard_map/while/body/eval_jaxpr/psum | solution.py:61
  509.9 7.5 collective-permute-start
  524.7 81.2 %all-reduce.6.cloned.1.call-done = f32[1,192,192]{2,1,0:T(8,128)} async-done(((f32[1,192,192]{2,1,0:T(8,128)}), f32[1,192,192]{2,1,0:T(8,128)}) %all-reduce.6.cloned.1.call-update) | async-done | bytes 147472 | tf_op jit(solution)/shard_map/while/body/eval_jaxpr/psum | solution.py:61
  607.5 7.5 collective-permute-start
  615.0 5.7 collective-permute-done
  622.3 81.1 %all-reduce.6.cloned.1.call-done = f32[1,192,192]{2,1,0:T(8,128)} async-done(((f32[1,192,192]{2,1,0:T(8,128)}), f32[1,192,192]{2,1,0:T(8,128)}) %all-reduce.6.cloned.1.call-update) | async-done | bytes 147472 | tf_op jit(solution)/shard_map/while/body/eval_jaxpr/psum | solution.py:61
  705.1 7.5 collective-permute-start
  719.9 81.2 %all-reduce.6.cloned.1.call-done = f32[1,192,192]{2,1,0:T(8,128)} async-done(((f32[1,192,192]{2,1,0:T(8,128)}), f32[1,192,192]{2,1,0:T(8,128)}) %all-reduce.6.cloned.1.call-update) | async-done | bytes 147472 | tf_op jit(solution)/shard_map/while/body/eval_jaxpr/psum | solution.py:61
  802.6 7.5 collective-permute-start
  817.4 81.2 %all-reduce.6.cloned.1.call-done = f32[1,192,192]{2,1,0:T(8,128)} async-done(((f32[1,192,192]{2,1,0:T(8,128)}), f32[1,192,192]{2,1,0:T(8,128)}) %all-reduce.6.cloned.1.call-update) | async-done | bytes 147472 | tf_op jit(solution)/shard_map/while/body/eval_jaxpr/psum | solution.py:61
  900.2 7.5 collective-permute-start
  907.7 5.7 collective-permute-done
  915.0 81.1 %all-reduce.6.cloned.1.call-done = f32[1,192,192]{2,1,0:T(8,128)} async-done(((f32[1,192,192]{2,1,0:T(8,128)}), f32[1,192,192]{2,1,0:T(8,128)}) %all-reduce.6.cloned.1.call-update) | async-done | bytes 147472 | tf_op jit(solution)/shard_map/while/body/eval_jaxpr/psum | solution.py:61
  997.8 7.5 collective-permute-start
  1005.3 5.7 collective-permute-done
  1012.6 81.2 %all-reduce.6.cloned.1.call-done = f32[1,192,192]{2,1,0:T(8,128)} async-done(((f32[1,192,192]{2,1,0:T(8,128)}), f32[1,192,192]{2,1,0:T(8,128)}) %all-reduce.6.cloned.1.call-update) | async-done | bytes 147472 | tf_op jit(solution)/shard_map/while/body/eval_jaxpr/psum | solution.py:61
  1095.4 7.5 collective-permute-start
  1102.9 5.7 collective-permute-done
  1110.2 81.2 %all-reduce.6.cloned.1.call-done = f32[1,192,192]{2,1,0:T(8,128)} async-done(((f32[1,192,192]{2,1,0:T(8,128)}), f32[1,192,192]{2,1,0:T(8,128)}) %all-reduce.6.cloned.1.call-update) | async-done | bytes 147472 | tf_op jit(solution)/shard_map/while/body/eval_jaxpr/psum | solution.py:61
  1193.0 7.5 collective-permute-start
  1200.5 5.7 collective-permute-done
  1207.8 81.2 %all-reduce.6.cloned.1.call-done = f32[1,192,192]{2,1,0:T(8,128)} async-done(((f32[1,192,192]{2,1,0:T(8,128)}), f32[1,192,192]{2,1,0:T(8,128)}) %all-reduce.6.cloned.1.call-update) | async-done | bytes 147472 | tf_op jit(solution)/shard_map/while/body/eval_jaxpr/psum | solution.py:61
  1290.5 7.5 collective-permute-start
  1305.3 81.2 %all-reduce.6.cloned.1.call-done = f32[1,192,192]{2,1,0:T(8,128)} async-done(((f32[1,192,192]{2,1,0:T(8,128)}), f32[1,192,192]{2,1,0:T(8,128)}) %all-reduce.6.cloned.1.call-update) | async-done | bytes 147472 | tf_op jit(solution)/shard_map/while/body/eval_jaxpr/psum | solution.py:61
  1388.1 7.5 collective-permute-start
  1402.9 81.2 %all-reduce.6.cloned.1.call-done = f32[1,192,192]{2,1,0:T(8,128)} async-done(((f32[1,192,192]{2,1,0:T(8,128)}), f32[1,192,192]{2,1,0:T(8,128)}) %all-reduce.6.cloned.1.call-update) | async-done | bytes 147472 | tf_op jit(solution)/shard_map/while/body/eval_jaxpr/psum | solution.py:61
  1485.7 7.5 collective-permute-start
  1500.5 81.2 %all-reduce.6.cloned.1.call-done = f32[1,192,192]{2,1,0:T(8,128)} async-done(((f32[1,192,192]{2,1,0:T(8,128)}), f32[1,192,192]{2,1,0:T(8,128)}) %all-reduce.6.cloned.1.call-update) | async-done | bytes 147472 | tf_op jit(solution)/shard_map/while/body/eval_jaxpr/psum | solution.py:61
  1583.2 7.5 collective-permute-start
  1598.0 81.2 %all-reduce.6.cloned.1.call-done = f32[1,192,192]{2,1,0:T(8,128)} async-done(((f32[1,192,192]{2,1,0:T(8,128)}), f32[1,192,192]{2,1,0:T(8,128)}) %all-reduce.6.cloned.1.call-update) | async-done | bytes 147472 | tf_op jit(solution)/shard_map/while/body/eval_jaxpr/psum | solution.py:61
  1696.1 77.3 %all-reduce.4.cloned.1.call-done = f32[192,192]{1,0:T(8,128)} async-done(((f32[192,192]{1,0:T(8,128)}), f32[192,192]{1,0:T(8,128)}) %all-reduce.4.cloned.1.call-update) | async-done | bytes 147472 | tf_op jit(solution)/shard_map/psum | solution.py:57
  1790.4 25.7 %psum.22 = f32[192,7]{1,0:T(8,128)S(1)} all-reduce(f32[192,7]{1,0:T(8,128)S(1)} %bitcast.59), channel_id=1, replica_groups=mesh['blk'=64,'dim'=8] {'dim'}, use_global_device_ids=true, to_apply=%region_9.10 | all-reduce | flops 1344 | bytes 10752 | tf_op jit(solution)/shard_map/psum | solution.py:57
  1817.6 14.4 scatter_custom_fusion.1
  1837.3 28.1 %all-to-all-start.2 = ((bf16[64,42,512]{2,1,0:T(8,128)(2,1)}), bf16[64,42,512]{2,1,0:T(8,128)(2,1)}, u32[]{:S(2)}, u32[]{:S(2)}) async-start(bf16[64,42,512]{2,1,0:T(8,128)(2,1)} %reshape.220), calls=%async_computation.2 | async-start | bytes 6291456 | tf_op jit(solution)/shard_map/all_to_all | solution.py:106
  1872.3 328.4 %while.25 = (s32[]{:T(128)}, f32[192,512]{1,0:T(8,128)S(1)}, s32[15]{0:T(128)S(1)}, bf16[192,3072]{1,0:T(8,128)(2,1)S(1)}, bf16[192,512]{1,0:T(8,128)(2,1)S(1)},...) while((s32[]{:T(128)}, f32[192,512]{1,0:T(8,128)S(1)}, s32[15]{0:T(128)S(1)}, ...), condition=%wide.region_14.15_spmd, body=%wide.region_13.14_spmd.sunk | while | flops 37847048 | bytes 2654423 | solution.py:126
  1879.0 6.9 collective-permute-done.1
  1887.4 5.9 collective-permute-start.1
  1893.4 121.8 %collective-permute-done.1 = f32[192,512]{1,0:T(8,128)S(1)} collective-permute-done((f32[192,512]{1,0:T(8,128)S(1)}, f32[192,512]{1,0:T(8,128)S(1)}, u32[]{:S(2)}, u32[]{:S(2)}) %collective-permute-start.1) | collective-permute-done | bytes 393248 | tf_op jit(solution)/shard_map/while/body/eval_jaxpr/ppermute | solution.py:16
  2018.7 10.8 collective-permute-done.1
  2033.0 10.8 collective-permute-done.1
  2047.2 10.8 collective-permute-done.1
  2061.5 10.8 collective-permute-done.1
  2075.8 10.8 collective-permute-done.1
  2090.1 10.8 collective-permute-done.1
  2104.3 10.8 collective-permute-done.1
  2118.6 10.8 collective-permute-done.1
  2132.9 10.8 collective-permute-done.1
  2147.1 10.8 collective-permute-done.1
  2161.4 10.8 collective-permute-done.1
  2175.7 10.8 collective-permute-done.1
  2189.9 10.8 collective-permute-done.1
  2211.0 20.8 scatter_custom_fusion.2
  (233 shorter events, 204.1 us)
Async XLA Ops:
  8.0 64.8 %copy-start = (bf16[384,512]{1,0:T(8,128)(2,1)S(1)}, bf16[384,512]{1,0:T(8,128)(2,1)}, u32[]{:S(2)}) copy-start(bf16[384,512]{1,0:T(8,128)(2,1)} %param.10) | copy-start | bytes 1179652
  72.6 8.8 copy-start.8
  83.9 5.7 copy-start.3
  83.9 5.8 copy-start.5
  83.9 6.7 copy-start.6
  83.9 1691.8 %all-to-all-start.1 = ((bf16[64,42,512]{2,1,0:T(8,128)(2,1)}), bf16[64,42,512]{2,1,0:T(8,128)(2,1)}, u32[]{:S(2)}, u32[]{:S(2)}) async-start(bf16[64,42,512]{2,1,0:T(8,128)(2,1)} %reshape.225), calls=%async_computation.1 | async-start | bytes 6291456 | tf_op jit(solution)/shard_map/all_to_all | solution.py:45
  90.5 222.6 %all-reduce.6.cloned.1.call-start = ((), (), s32[]{:S(2)}) async-start(), calls=%async_computation.4 | async-start | bytes 393216 | tf_op jit(solution)/shard_map/while/body/eval_jaxpr/psum | solution.py:61
  90.5 10.7 collective-permute-start
  314.8 96.0 %all-reduce.6.cloned.1.call-start = ((), (), s32[]{:S(2)}) async-start(), calls=%async_computation.4 | async-start | bytes 393216 | tf_op jit(solution)/shard_map/while/body/eval_jaxpr/psum | solution.py:61
  314.8 13.1 collective-permute-start
  412.4 96.0 %all-reduce.6.cloned.1.call-start = ((), (), s32[]{:S(2)}) async-start(), calls=%async_computation.4 | async-start | bytes 393216 | tf_op jit(solution)/shard_map/while/body/eval_jaxpr/psum | solution.py:61
  412.4 13.1 collective-permute-start
  509.9 96.0 %all-reduce.6.cloned.1.call-start = ((), (), s32[]{:S(2)}) async-start(), calls=%async_computation.4 | async-start | bytes 393216 | tf_op jit(solution)/shard_map/while/body/eval_jaxpr/psum | solution.py:61
  509.9 13.1 collective-permute-start
  607.5 95.9 %all-reduce.6.cloned.1.call-start = ((), (), s32[]{:S(2)}) async-start(), calls=%async_computation.4 | async-start | bytes 393216 | tf_op jit(solution)/shard_map/while/body/eval_jaxpr/psum | solution.py:61
  607.5 13.1 collective-permute-start
  705.1 95.9 %all-reduce.6.cloned.1.call-start = ((), (), s32[]{:S(2)}) async-start(), calls=%async_computation.4 | async-start | bytes 393216 | tf_op jit(solution)/shard_map/while/body/eval_jaxpr/psum | solution.py:61
  705.1 13.1 collective-permute-start
  802.6 96.0 %all-reduce.6.cloned.1.call-start = ((), (), s32[]{:S(2)}) async-start(), calls=%async_computation.4 | async-start | bytes 393216 | tf_op jit(solution)/shard_map/while/body/eval_jaxpr/psum | solution.py:61
  802.6 13.1 collective-permute-start
  900.2 95.9 %all-reduce.6.cloned.1.call-start = ((), (), s32[]{:S(2)}) async-start(), calls=%async_computation.4 | async-start | bytes 393216 | tf_op jit(solution)/shard_map/while/body/eval_jaxpr/psum | solution.py:61
  900.2 13.1 collective-permute-start
  997.8 96.0 %all-reduce.6.cloned.1.call-start = ((), (), s32[]{:S(2)}) async-start(), calls=%async_computation.4 | async-start | bytes 393216 | tf_op jit(solution)/shard_map/while/body/eval_jaxpr/psum | solution.py:61
  997.8 13.1 collective-permute-start
  1095.4 96.0 %all-reduce.6.cloned.1.call-start = ((), (), s32[]{:S(2)}) async-start(), calls=%async_computation.4 | async-start | bytes 393216 | tf_op jit(solution)/shard_map/while/body/eval_jaxpr/psum | solution.py:61
  1095.4 13.1 collective-permute-start
  1193.0 96.0 %all-reduce.6.cloned.1.call-start = ((), (), s32[]{:S(2)}) async-start(), calls=%async_computation.4 | async-start | bytes 393216 | tf_op jit(solution)/shard_map/while/body/eval_jaxpr/psum | solution.py:61
  1193.0 13.1 collective-permute-start
  1290.5 96.0 %all-reduce.6.cloned.1.call-start = ((), (), s32[]{:S(2)}) async-start(), calls=%async_computation.4 | async-start | bytes 393216 | tf_op jit(solution)/shard_map/while/body/eval_jaxpr/psum | solution.py:61
  1290.5 13.1 collective-permute-start
  1388.1 95.9 %all-reduce.6.cloned.1.call-start = ((), (), s32[]{:S(2)}) async-start(), calls=%async_computation.4 | async-start | bytes 393216 | tf_op jit(solution)/shard_map/while/body/eval_jaxpr/psum | solution.py:61
  1388.1 13.1 collective-permute-start
  1485.7 96.0 %all-reduce.6.cloned.1.call-start = ((), (), s32[]{:S(2)}) async-start(), calls=%async_computation.4 | async-start | bytes 393216 | tf_op jit(solution)/shard_map/while/body/eval_jaxpr/psum | solution.py:61
  1485.7 13.1 collective-permute-start
  1583.2 96.0 %all-reduce.6.cloned.1.call-start = ((), (), s32[]{:S(2)}) async-start(), calls=%async_computation.4 | async-start | bytes 393216 | tf_op jit(solution)/shard_map/while/body/eval_jaxpr/psum | solution.py:61
  1583.2 13.1 collective-permute-start
  1680.8 92.6 %all-reduce.4.cloned.1.call-start = ((), (), s32[]{:S(2)}) async-start(), calls=%async_computation.3 | async-start | bytes 393216 | tf_op jit(solution)/shard_map/psum | solution.py:57
  1689.6 83.8 %copy-start.1 = (f32[192,2880]{1,0:T(8,128)}, f32[192,2880]{1,0:T(8,128)S(1)}, u32[]{:S(2)}) copy-start(f32[192,2880]{1,0:T(8,128)S(1)} %reshape.213) | copy-start | bytes 6635524
  1788.1 28.1 %copy-start.10 = (f32[192]{0:T(256)S(1)}, f32[192]{0:T(256)}, u32[]{:S(2)}) copy-start(f32[192]{0:T(256)} %fusion.8) | copy-start | bytes 2308
  1788.1 28.4 %copy-start.2 = (f32[192,2880]{1,0:T(8,128)S(1)}, f32[192,2880]{1,0:T(8,128)}, u32[]{:S(2)}) copy-start(f32[192,2880]{1,0:T(8,128)} %copy-done.1) | copy-start | bytes 6635524
  1788.1 28.4 %copy-start.7 = (f32[192,192]{1,0:T(8,128)S(1)}, f32[192,192]{1,0:T(8,128)}, u32[]{:S(2)}) copy-start(f32[192,192]{1,0:T(8,128)} %all-reduce.4.cloned.1.call-done) | copy-start | bytes 442372
  1837.3 368.0 %all-to-all-start.2 = ((bf16[64,42,512]{2,1,0:T(8,128)(2,1)}), bf16[64,42,512]{2,1,0:T(8,128)(2,1)}, u32[]{:S(2)}, u32[]{:S(2)}) async-start(bf16[64,42,512]{2,1,0:T(8,128)(2,1)} %reshape.220), calls=%async_computation.2 | async-start | bytes 6291456 | tf_op jit(solution)/shard_map/all_to_all | solution.py:106
  1865.4 4.4 copy-start.9
  1873.9 12.0 collective-permute-start.1
  1887.4 127.8 %collective-permute-start.1 = (f32[192,512]{1,0:T(8,128)S(1)}, f32[192,512]{1,0:T(8,128)S(1)}, u32[]{:S(2)}, u32[]{:S(2)}) collective-permute-start(f32[192,512]{1,0:T(8,128)S(1)} %convolution_add_fusion.4), channel_id=1, source_target_pairs={{0,8},{8,16},{16,24},{24,32},{32,40},{40,48},{48,56},{56,64},{64,7... | collective-permute-start | bytes 1179656 | tf_op jit(solution)/shard_map/while/body/eval_jaxpr/ppermute | solution.py:16
  2016.8 12.7 collective-permute-start.1
  2031.0 12.7 collective-permute-start.1
  2045.3 12.7 collective-permute-start.1
  2059.6 12.7 collective-permute-start.1
  2073.9 12.7 collective-permute-start.1
  2088.1 12.7 collective-permute-start.1
  2102.4 12.7 collective-permute-start.1
  2116.7 12.7 collective-permute-start.1
  2130.9 12.7 collective-permute-start.1
  2145.2 12.7 collective-permute-start.1
  2159.5 12.7 collective-permute-start.1
  2173.7 12.7 collective-permute-start.1
  2188.0 12.7 collective-permute-start.1
  2200.7 3.1 copy-start.4
Sparse Core Ops, SparseCore 0:
  102.3 210.8 all-reduce.5
  329.0 81.7 all-reduce.5
  426.6 81.7 all-reduce.5
  524.1 81.7 all-reduce.5
  621.7 81.6 all-reduce.5
  719.3 81.6 all-reduce.5
  816.8 81.7 all-reduce.5
  914.4 81.6 all-reduce.5
  1012.0 81.7 all-reduce.5
  1109.6 81.7 all-reduce.5
  1207.2 81.7 all-reduce.5
  1304.7 81.7 all-reduce.5
  1402.3 81.6 all-reduce.5
  1499.9 81.7 all-reduce.5
  1597.4 81.7 all-reduce.5
Sparse Core Ops, SparseCore 1:
  1684.7 88.6 all-reduce.3
where the time goes:
time: 2250 us; the launch traced here: 2240 us
  waiting for transfers between devices  1780 us (79%)
  starting transfers between devices  177 us (8%)
  local copies, waits for them, and re-layouts  104 us (5%)
  other arithmetic  64.5 us (3%)
  blocking collectives  60 us (3%)
  matrix products  26.1 us (1%)
    psum x15, waiting for transfers between devices, scored_step(): lax.psum(jnp.dot(queries, following.T, preferred_element_type=jnp.float32...  1350 us
    ppermute x30, waiting for transfers between devices, shifted(): return lax.ppermute(value, axis, pairs)  356 us
    ppermute x30, starting transfers between devices, shifted(): return lax.ppermute(value, axis, pairs)  143 us
    psum x1, waiting for transfers between devices, on_device(): first_tile, mined_foil_logits = lax.psum((own_tile, hard_part), 'dim')  77.3 us
  transfers between devices with their start and end apart: 48, of which 46 were waited for; matrix products, arithmetic and copies ran while one was open for 4% of the time, Pallas kernels for 0%

commit v1 on v0

v1 whole, which is shorter than its diff:
```python
import functools

import jax
import jax.numpy as jnp
from jax import lax
from jax.experimental import pallas as pl
from jax.experimental.pallas import tpu as pltpu
from jax.sharding import PartitionSpec as P

WINDOW = 16
HARD = 7
PLANE = 4
REACH = WINDOW // PLANE
SUB = 2
LOW = -1e30

logit_divisor = 0.02
scale = 1.0 / logit_divisor

F32, BF16 = jnp.float32, jnp.bfloat16
MESH = pl.DeviceIdType.MESH


def dot(left, right, left_dim, right_dim):
    return lax.dot_general(
        left, right, (((left_dim,), (right_dim,)), ((), ())), preferred_element_type=F32
    )


def remote(src, dst, send_sem, recv_sem, device):
    return pltpu.make_async_remote_copy(
        src_ref=src,
        dst_ref=dst,
        send_sem=send_sem,
        recv_sem=recv_sem,
        device_id=device,
        device_id_type=MESH,
    )


def loop(low, high, body):
    def step(index, carry):
        body(index)
        return carry

    lax.fori_loop(low, high, step, 0)


def kernel(
    planes, dims,
    q_in, p_in, n_in, idx_in, gq_out, dp_out, dn_out,
    qbuf, idxb, pbuf, nbuf, qcat, st, rbuf, sc, hp, hrecv, wsend, wrecv, msg, arecv, hwb,
    wt, wht, cbuf, win, dnb, dpb, recva, recvb, senda, sendb, csend, crecv, ysend, yrecv,
    loc, us, ur, ds, dr, ps, pr, ns, nr, rss, rsr, hss, hsr, wss, wsr, ags, agr, hws, hwr,
    wts, wtr, as_, ar, bs, br, cs, cr, ys, yr,
):
    rows, feats = q_in.shape
    pool = n_in.shape[0]
    wide = PLANE * rows
    lanes = hwb.shape[2]
    chunk = wide // dims
    half = planes // 2
    part = rows // SUB

    b = lax.axis_index("blk")
    e = lax.axis_index("dim")
    z = lax.div(b, PLANE)
    yc = lax.rem(b, PLANE)
    core_yc = yc + 1 - 2 * lax.rem(yc, 2)
    far_yc = lax.rem(yc + 2, PLANE)
    cross_yc = PLANE - 1 - yc

    def at_plane(step):
        return (lax.rem(z + step + planes, planes) * PLANE + yc, e)

    def at_dim(p):
        return (b, lax.rem(e + p, dims))

    core = (z * PLANE + core_yc, e)
    far = (z * PLANE + far_yc, e)
    up, down = at_plane(1), at_plane(-1)

    def take(y, size):
        return pl.ds(pl.multiple_of(y * size, 32), size)

    own = [
        pltpu.make_async_copy(q_in, qbuf.at[0], loc.at[0]),
        pltpu.make_async_copy(p_in, pbuf.at[take(yc, rows)], loc.at[1]),
        pltpu.make_async_copy(n_in, nbuf.at[take(yc, pool)], loc.at[2]),
        pltpu.make_async_copy(idx_in, idxb.at[0], loc.at[3]),
    ]
    for copy in own:
        copy.start()
    barrier = pltpu.get_barrier_semaphore()
    met = [at_plane(s) for s in range(1, planes)] + [core, far]
    met += [at_dim(p) for p in range(1, dims)]
    for device in met:
        pl.semaphore_signal(barrier, inc=1, device_id=device, device_id_type=MESH)
    hp[...] = jnp.zeros_like(hp)
    dnb[...] = jnp.zeros_like(dnb)
    recva[0] = jnp.zeros((rows, feats), BF16)
    recvb[0] = jnp.zeros((rows, feats), BF16)
    for copy in own:
        copy.wait()
    pl.semaphore_wait(barrier, len(met))

    def up_copy(s, i):
        if i == SUB:
            return remote(idxb.at[s - 1], idxb.at[s], us.at[s, i], ur.at[s, i], up)
        at = pl.ds(i * part, part)
        return remote(qbuf.at[s - 1, at], qbuf.at[s, at], us.at[s, i], ur.at[s, i], up)

    def down_copy(s, i):
        src = jnp.where(s == 1, 0, half + s - 1)
        if i == SUB:
            return remote(idxb.at[src], idxb.at[half + s], ds.at[s, i], dr.at[s, i], down)
        at = pl.ds(i * part, part)
        return remote(qbuf.at[src, at], qbuf.at[half + s, at], ds.at[s, i], dr.at[s, i], down)

    def plane_copy(buf, size, sends, recvs, i):
        at = take(far_yc if i == 2 else yc, size)
        return remote(buf.at[at], buf.at[at], sends.at[i], recvs.at[i], far if i == 1 else core)

    p_copy = functools.partial(plane_copy, pbuf, rows, ps, pr)
    n_copy = functools.partial(plane_copy, nbuf, pool, ns, nr)

    for i in range(SUB + 1):
        up_copy(1, i).start()
        down_copy(1, i).start()
    for i in (1, 0):
        p_copy(i).start()
        n_copy(i).start()

    sub = lax.broadcasted_iota(jnp.int32, (8, rows), 0)

    def named(j):
        ids = idxb[j, :, 0:rows] - z * (PLANE * pool)
        low, high = ids & 7, ids >> 3
        keys = [jnp.where(low[k : k + 1] == sub, high[k : k + 1], -1) for k in range(HARD)]
        return ids, keys

    def hard_copy(j):
        step = jnp.where(j <= half, -j, j - half)
        return remote(hp.at[j], hrecv.at[j], hss.at[j], hsr.at[j], at_plane(step))

    def scored(t):
        s = lax.div(t + 1, 2)
        j = jnp.where(lax.rem(t, 2) == 1, s, jnp.where(t == 0, 0, half + s))
        query = qbuf[j]
        ids, keys = named(j)

        def one(y, acc):
            scores = dot(nbuf[take(y, pool)], query, 1, 1)
            base = y * (pool // 8)
            acc = list(acc)
            for r in range(pool // 8):
                tile = scores[8 * r : 8 * r + 8]
                for k in range(HARD):
                    acc[k] = jnp.where(keys[k] == base + r, tile, acc[k])
            return tuple(acc)

        acc = lax.fori_loop(0, PLANE, one, (jnp.zeros((8, rows), F32),) * HARD)
        out = jnp.zeros((8, rows), F32)
        for k in range(HARD):
            out = jnp.where(sub == k, jnp.sum(acc[k], axis=0, keepdims=True), out)
        hp[j, :, 0:rows] = out

        @pl.when(j > 0)
        def _():
            hard_copy(j).start()

    def score_copy(p):
        at = take(lax.rem(e + p, dims), chunk)
        return remote(st.at[at], rbuf.at[p], rss.at[p], rsr.at[p], at_dim(p))

    def version(y):
        return jnp.where(y >= yc, 0, 1)

    def window_scores():
        qcat[0, 0:rows] = qbuf[0]
        qcat[1, 0:rows] = qbuf[REACH]
        for v in range(2):
            for g in range(1, REACH):
                qcat[v, g * rows : (g + 1) * rows] = qbuf[g]

        def one(y):
            at = take(y, rows)
            st[at] = dot(pbuf[at], qcat[version(y)], 1, 1)

        loop(0, PLANE, one)
        for p in range(1, dims):
            score_copy(p).start()

    first, jobs = (3, 3) if half >= 8 else (1, 2)

    def ring_step(s):
        for i in range(SUB + 1):
            up_copy(s, i).wait_recv()

            @pl.when(s < half)
            def _():
                up_copy(s + 1, i).start()
                down_copy(s, i).wait_recv()

            @pl.when(s < half - 1)
            def _():
                down_copy(s + 1, i).start()

        @pl.when(s == first)
        def _():
            for copy in (p_copy, n_copy):
                copy(1).wait_recv()
                copy(2).start()
            for copy in (n_copy, p_copy):
                copy(0).wait_recv()
                copy(2).wait_recv()

        @pl.when(s == REACH)
        def _():
            window_scores()

        @pl.when(s >= first)
        def _():
            low = jobs * (s - first)
            loop(low, jnp.minimum(low + jobs, planes), scored)

    loop(1, half + 1, ring_step)

    total = st[take(e, chunk)]
    for p in range(1, dims):
        score_copy(p).wait_recv()
        total = total + rbuf[p]
    total = total * scale
    sc[...] = total
    top = jnp.max(total, axis=0, keepdims=True)
    part_lse = top + jnp.log(jnp.sum(jnp.exp(total - top), axis=0, keepdims=True))
    part_lse = jnp.broadcast_to(part_lse, (8, wide))
    owner = lax.div(e * chunk, rows)
    ahead = jnp.full((8, lanes), owner, jnp.int32) >= yc

    def lse_copy(g):
        return remote(wsend.at[g], wrecv.at[g], wss.at[g], wsr.at[g], at_plane(-g))

    wsend[0] = jnp.where(ahead, part_lse[:, :lanes], LOW)
    wsend[REACH] = jnp.where(ahead, LOW, part_lse[:, :lanes])
    for g in range(1, REACH):
        wsend[g] = pltpu.roll(part_lse, wide - g * rows, 1)[:, :lanes]
    for g in range(REACH, 0, -1):
        lse_copy(g).start()

    hard_sum = hp[0]
    for j in range(1, planes):
        hard_copy(j).wait_recv()
        hard_sum = hard_sum + hrecv[j]
    parts = [wsend[0]]
    for g in range(1, REACH + 1):
        lse_copy(g).wait_recv()
        parts.append(wrecv[g])

    def joined(values):
        highest = functools.reduce(jnp.maximum, values)
        return highest + jnp.log(sum(jnp.exp(value - highest) for value in values))

    last = lax.broadcasted_iota(jnp.int32, (8, lanes), 0) == HARD
    msg[...] = jnp.where(last, joined(parts), hard_sum)

    def sum_copy(p):
        return remote(msg, arecv.at[p], ags.at[p], agr.at[p], at_dim(p))

    for p in range(1, dims):
        sum_copy(p).start()
    values = [msg[...]]
    for p in range(1, dims):
        sum_copy(p).wait_recv()
        values.append(arecv[p])
    entries = jnp.where(last, joined(values), sum(values) * scale)
    highest = jnp.max(entries, axis=0, keepdims=True)
    log_total = highest + jnp.log(jnp.sum(jnp.exp(entries - highest), axis=0, keepdims=True))
    hard_weights = jnp.exp(entries - log_total).astype(BF16).astype(F32)
    hwb[0] = jnp.where(last, log_total, hard_weights)

    def weight_copy(j):
        step = jnp.where(j <= half, j, half - j)
        return remote(hwb.at[0], hwb.at[j], hws.at[j], hwr.at[j], at_plane(step))

    loop(1, planes, lambda j: weight_copy(j).start())

    lane = lax.broadcasted_iota(jnp.int32, (8, wide), 1)
    logs = jnp.zeros((8, wide), F32)
    for g in range(REACH):
        if g == 0:
            weight_copy(REACH).wait_recv()
            one_log = jnp.where(ahead, hwb[0, HARD : HARD + 1], hwb[REACH, HARD : HARD + 1])
        else:
            weight_copy(g).wait_recv()
            one_log = jnp.broadcast_to(hwb[g, HARD : HARD + 1], (8, lanes))
        if wide > lanes:
            one_log = jnp.concatenate([one_log, jnp.zeros((8, wide - lanes), F32)], axis=1)
        if g > 0:
            one_log = pltpu.roll(one_log, g * rows, 1)
        logs = jnp.where((lane >= g * rows) & (lane < (g + 1) * rows), one_log, logs)
    row_at = lax.broadcasted_iota(jnp.int32, (chunk, wide), 0) + lax.rem(e * chunk, rows)
    lane_at = lax.broadcasted_iota(jnp.int32, (chunk, wide), 1)
    positive = (row_at == lane_at) & (jnp.full((chunk, wide), owner, jnp.int32) == yc)
    weights = jnp.exp(sc[...] - logs[0:1]) - jnp.where(positive, 1.0, 0.0)
    wt[take(e, chunk)] = weights.astype(BF16)

    def tile_copy(p):
        at = take(e, chunk)
        return remote(wt.at[at], wt.at[at], wts.at[p], wtr.at[p], at_dim(p))

    for p in range(1, dims):
        tile_copy(p).start()

    def graded(u):
        t = lax.div(u, 2)
        j = jnp.where(lax.rem(u, 2) == 0, half - t, planes - 1 - t)
        j = jnp.where(u == planes - 1, 0, j)

        @pl.when(j > REACH)
        def _():
            weight_copy(j).wait_recv()

        query = qbuf[j]
        ids, keys = named(j)
        pay = hwb[j, :, 0:rows]
        merged = []
        for k in range(HARD):
            same = jnp.where(ids == ids[k : k + 1], pay, 0.0)
            same = jnp.where(sub < HARD, same, 0.0)
            merged.append(jnp.broadcast_to(jnp.sum(same, axis=0, keepdims=True), (8, rows)))

        def one(y):
            base = y * (pool // 8)
            for r in range(pool // 16):
                pair = []
                for i in range(2):
                    tile = jnp.zeros((8, rows), F32)
                    for k in range(HARD):
                        tile = jnp.where(keys[k] == base + (2 * r + i), merged[k], tile)
                    pair.append(tile)
                at = pl.ds(pl.multiple_of(y * pool + 16 * r, 16), 16)
                wht[at] = jnp.concatenate(pair, axis=0).astype(BF16)
            at = take(y, pool)
            dnb[at] += dot(wht[at], query, 1, 0)

        loop(0, PLANE, one)
        cbuf[j] = dot(wht[...], nbuf[...], 0, 0)

    def window_grads():
        for p in range(1, dims):
            tile_copy(p).wait_recv()
        near = jnp.zeros((lanes, feats), F32)
        rest = jnp.zeros((lanes, feats), F32)
        for y in range(PLANE):
            at = pl.ds(y * rows, rows)
            dpb[at] = dot(wt[at], qcat[version(y)], 1, 0)
            piece = dot(wt[at, 0:lanes], pbuf[at], 0, 0)
            here = jnp.full((lanes, feats), y, jnp.int32) >= yc
            near = near + jnp.where(here, piece, 0.0)
            rest = rest + jnp.where(here, 0.0, piece)
        win[0:lanes] = near + rest
        win[0:rows] = near[0:rows]
        win[REACH * rows : (REACH + 1) * rows] = rest[0:rows]
        if wide > lanes:
            win[lanes:wide] = dot(wt[:, lanes:wide], pbuf[...], 0, 0)

    def a_copy(t):
        return remote(senda.at[t], recva.at[t + 1], as_.at[t + 1], ar.at[t + 1], down)

    def b_copy(t):
        return remote(sendb.at[t], recvb.at[t + 1], bs.at[t + 1], br.at[t + 1], up)

    c_copy = remote(csend, crecv, cs.at[0], cr.at[0], core)
    y_copy = remote(ysend, yrecv, ys.at[0], yr.at[0], far)

    def core_stage():
        for i, y in enumerate((core_yc, cross_yc)):
            csend[i, 0:pool] = dnb[take(y, pool)].astype(BF16)
            csend[i, pool : pool + rows] = dpb[take(y, rows)].astype(BF16)
        c_copy.start()

    def far_stage():
        c_copy.wait_recv()
        ysend[0:pool] = (dnb[take(far_yc, pool)] + crecv[1, 0:pool].astype(F32)).astype(BF16)
        other = dpb[take(far_yc, rows)] + crecv[1, pool : pool + rows].astype(F32)
        ysend[pool : pool + rows] = other.astype(BF16)
        y_copy.start()

    done_at = -(-(planes - 5) // 3)

    def back_step(t):
        ja = half - t

        @pl.when(t > 0)
        def _():
            a_copy(t - 1).wait_recv()

        @pl.when(ja > REACH)
        def _():
            senda[t] = (cbuf[ja] + recva[t].astype(F32)).astype(BF16)

        @pl.when(ja <= REACH)
        def _():
            piece = cbuf[ja] + win[take(ja, rows)]
            senda[t] = (piece + recva[t].astype(F32)).astype(BF16)

        a_copy(t).start()

        @pl.when(t < half - 1)
        def _():
            @pl.when(t > 0)
            def _():
                b_copy(t - 1).wait_recv()

            sendb[t] = (cbuf[planes - 1 - t] + recvb[t].astype(F32)).astype(BF16)
            b_copy(t).start()

        loop(jnp.minimum(2 + 3 * t, planes), jnp.minimum(5 + 3 * t, planes), graded)
        if half > REACH:
            pl.when(t == half - REACH - 1)(window_grads)
        pl.when(t == done_at)(core_stage)
        pl.when(t == done_at + 1)(far_stage)

    loop(0, 2, graded)
    if half <= REACH:
        window_grads()
    loop(0, half, back_step)

    a_copy(half - 1).wait_recv()
    b_copy(half - 2).wait_recv()
    back = recva[half].astype(F32) + recvb[half - 1].astype(F32)
    gq_out[...] = (cbuf[0] + win[0:rows] + back) * scale
    y_copy.wait_recv()
    back = crecv[0].astype(F32) + yrecv[...].astype(F32)
    dn_out[...] = (dnb[take(yc, pool)] + back[0:pool]) * scale
    dp_out[...] = (dpb[take(yc, rows)] + back[pool : pool + rows]) * scale

    for i in range(SUB + 1):
        loop(1, half + 1, lambda s: up_copy(s, i).wait_send())
        loop(1, half, lambda s: down_copy(s, i).wait_send())
    for i in range(3):
        p_copy(i).wait_send()
        n_copy(i).wait_send()
    for p in range(1, dims):
        score_copy(p).wait_send()
        sum_copy(p).wait_send()
        tile_copy(p).wait_send()
    for g in range(1, REACH + 1):
        lse_copy(g).wait_send()
    loop(1, planes, lambda j: hard_copy(j).wait_send())
    loop(1, planes, lambda j: weight_copy(j).wait_send())
    loop(0, half, lambda t: a_copy(t).wait_send())
    loop(0, half - 1, lambda t: b_copy(t).wait_send())
    c_copy.wait_send()
    y_copy.wait_send()


def on_device(queries, passages, negatives, hard_index):
    rows, feats = queries.shape
    pool = negatives.shape[0]
    planes = lax.axis_size("blk") // PLANE
    dims = lax.axis_size("dim")
    half = planes // 2
    wide = PLANE * rows
    chunk = wide // dims
    lanes = -(-rows // 128) * 128
    both = pool + rows
    index = jnp.pad(hard_index.T, ((0, 8 - HARD), (0, lanes - rows)), constant_values=-1)

    dma = pltpu.SemaphoreType.DMA
    vmem = pltpu.VMEM
    scratch = [
        vmem((planes, rows, feats), BF16),
        vmem((planes, 8, lanes), jnp.int32),
        vmem((wide, feats), BF16),
        vmem((PLANE * pool, feats), BF16),
        vmem((2, wide, feats), BF16),
        vmem((wide, wide), F32),
        vmem((dims, chunk, wide), F32),
        vmem((chunk, wide), F32),
        vmem((planes, 8, lanes), F32),
        vmem((planes, 8, lanes), F32),
        vmem((REACH + 1, 8, lanes), F32),
        vmem((REACH + 1, 8, lanes), F32),
        vmem((8, lanes), F32),
        vmem((dims, 8, lanes), F32),
        vmem((planes, 8, lanes), F32),
        vmem((wide, wide), BF16),
        vmem((PLANE * pool, rows), BF16),
        vmem((planes, rows, feats), F32),
        vmem(((REACH + 1) * rows, feats), F32),
        vmem((PLANE * pool, feats), F32),
        vmem((wide, feats), F32),
        vmem((half + 1, rows, feats), BF16),
        vmem((half, rows, feats), BF16),
        vmem((half, rows, feats), BF16),
        vmem((half - 1, rows, feats), BF16),
        vmem((2, both, feats), BF16),
        vmem((2, both, feats), BF16),
        vmem((both, feats), BF16),
        vmem((both, feats), BF16),
        dma((4,)),
    ]
    for shape in (
        (half + 1, SUB + 1), (half, SUB + 1), (3,), (3,), (dims,), (planes,), (REACH + 1,),
        (dims,), (planes,), (dims,), (half + 1,), (half,), (1,), (1,),
    ):
        scratch += [dma(shape), dma(shape)]

    return pl.pallas_call(
        functools.partial(kernel, planes, dims),
        out_shape=(
            jax.ShapeDtypeStruct((rows, feats), F32),
            jax.ShapeDtypeStruct((rows, feats), F32),
            jax.ShapeDtypeStruct((pool, feats), F32),
        ),
        in_specs=[pl.BlockSpec(memory_space=pl.ANY)] * 4,
        out_specs=[pl.BlockSpec(memory_space=pltpu.VMEM)] * 3,
        scratch_shapes=scratch,
        compiler_params=pltpu.CompilerParams(
            collective_id=0, has_side_effects=True, vmem_limit_bytes=60 * 1024 * 1024
        ),
    )(queries, passages, negatives, index)


def solution(mesh):
    placed = (P("blk", "dim"), P("blk", "dim"), P("blk", "dim"), P("blk", None))
    return jax.shard_map(
        on_device,
        mesh=mesh,
        in_specs=placed,
        out_specs=(P("blk", "dim"), P("blk", "dim"), P("blk", "dim")),
        check_vma=False,
    )
```

time: 2250 us -> 162 us (0.07)
  waiting for transfers between devices: 1780 us -> 0 us
  starting transfers between devices: 177 us -> 0 us
  Pallas kernels: 0 us -> 156 us
  local copies, waits for them, and re-layouts: 104 us -> 5.79 us
  other arithmetic: 64.5 us -> 0 us
  blocking collectives: 60 us -> 0 us
  matrix products: 26.1 us -> 0 us
    psum x16 -> x0, waiting for transfers between devices: 1420 us -> none  [the longest x15 1350 us: scored_step(): lax.psum(jnp.dot(queries, following.T, preferred_element_type=jnp.float32...]
    ppermute x30 -> x0, waiting for transfers between devices: 356 us -> none  [shifted(): return lax.ppermute(value, axis, pairs)]
    pallas_call x0 -> x1, Pallas kernels: none -> 156 us  [on_device(): pl.pallas_call(functools.partial(kernel, planes, dims), out_shape=(jax.Sh...]
    ppermute x30 -> x0, starting transfers between devices: 143 us -> none  [shifted(): return lax.ppermute(value, axis, pairs)]
    dynamic_update_slice x30 -> x0, local copies, waits for them, and re-layouts: 34.6 us -> none  [on_device(): lax.scan(scored_step, passages, None, length=WINDOW - 1)]
    all_to_all x1 -> x0, blocking collectives: 34.3 us -> none  [on_device(): lax.all_to_all(wanted, 'blk', split_axis=0, concat_axis=0, tiled=True)]
    all_to_all x2 -> x0, starting transfers between devices: 33.8 us -> none  [the longest x1 28.1 us: on_device(): lax.all_to_all(outgoing.reshape(blocks, capacity, feature_width), 'blk',...]
    dot_general x35 -> x0, matrix products: 26.1 us -> none  [the longest x15 13.6 us: scored_step(): jnp.dot(queries, following.T, preferred_element_type=jnp.float32)]
  transfers between devices with their start and end apart: 48 -> 0, of which waited for: 46 -> 0; matrix products, arithmetic and copies ran while one was open for 4% -> 0% of each run, Pallas kernels for 0% -> 0%
where the time goes in v1:
time: 162 us
  Pallas kernels  156 us (96%)
  local copies, waits for them, and re-layouts  5.79 us (4%)
    pallas_call x1, Pallas kernels, on_device(): pl.pallas_call(functools.partial(kernel, planes, dims), out_shape=(jax.Sh...  156 us
    unnamed x5, local copies, waits for them, and re-layouts  4.49 us

profile of v1, /device:TPU:1, one launch (start us, length us, event | category | flops | bytes accessed | tf_op | source)
XLA Modules:
  0.0 162.2 jit_solution(17659232682634048938)
XLA Ops:
  0.6 1.3 pad.4.idx_in
  1.9 155.8 %shard_map.67 = (f32[192,512]{1,0:T(8,128)}, f32[192,512]{1,0:T(8,128)}, f32[384,512]{1,0:T(8,128)}) custom-call(bf16[192,512]{1,0:T(8,128)(2,1)} %q_in.1, bf16[192,512]{1,0:T(8,128)(2,1)} %p_in.1, bf16[384,512]{1,0:T(8,128)(2,1)} %n_in.1, s32[8,256]{1,0:T(8,128)} %pad.4.idx_in), custom_call_target="tpu_custom_call" | custom-call | tf_op jit(solution)/shard_map/pallas_call | solution.py:511
  157.7 0.0 copy-start
  157.7 1.8 %copy.10 = f32[192,512]{1,0:T(8,128)} copy(f32[192,512]{1,0:T(8,128)} %get-tuple-element.6) | data formatting | bytes 786432
  159.5 1.8 %copy.11 = f32[192,512]{1,0:T(8,128)} copy(f32[192,512]{1,0:T(8,128)} %get-tuple-element.7) | data formatting | bytes 786432
  161.3 0.0 copy-done
  161.3 0.9 copy.12
Async XLA Ops:
  157.7 3.6 %copy-start = (f32[384,512]{1,0:T(8,128)S(1)}, f32[384,512]{1,0:T(8,128)}, u32[]{:S(2)}) copy-start(f32[384,512]{1,0:T(8,128)} %get-tuple-element.8) | copy-start | bytes 2359300

commit v2 on v1

v2 whole, which is shorter than its diff:
```python
import functools

import jax
import jax.numpy as jnp
from jax import lax
from jax.experimental import pallas as pl
from jax.experimental.pallas import tpu as pltpu
from jax.sharding import PartitionSpec as P

WINDOW = 16
HARD = 7
PLANE = 4
DIM_Y = 2
REACH = WINDOW // PLANE
SUB = 2
LOW = -1e30

logit_divisor = 0.02
scale = 1.0 / logit_divisor

F32, BF16 = jnp.float32, jnp.bfloat16
MESH = pl.DeviceIdType.MESH


def dot(left, right, left_dim, right_dim):
    return lax.dot_general(
        left, right, (((left_dim,), (right_dim,)), ((), ())), preferred_element_type=F32
    )


def remote(src, dst, send_sem, recv_sem, device):
    return pltpu.make_async_remote_copy(
        src_ref=src,
        dst_ref=dst,
        send_sem=send_sem,
        recv_sem=recv_sem,
        device_id=device,
        device_id_type=MESH,
    )


def loop(low, high, body):
    def step(index, carry):
        body(index)
        return carry

    lax.fori_loop(low, high, step, 0)


def kernel(
    planes, dims,
    q_in, p_in, n_in, idx_in, gq_out, dp_out, dn_out,
    qbuf, idxb, idxp, pbuf, nbuf, qcat, st, relay, merged, nextto, mine, ysum, yget, sc,
    hp, hrecv, wsend, wrecv, msg, arecv, hwb, wt, wht, cbuf, win, dnb, dpb,
    recva, recvb, senda, sendb, nsend, nrecv, psend, precv, nfar, ngot, pfar, pgot,
    loc, us, ur, ds, dr, ps, pr, ns, nr, xs, xr, ls, lr, hss, hsr, wss, wsr, ags, agr,
    hws, hwr, wts, wtr, as_, ar, bs, br, cs, cr, ys, yr,
):
    rows, feats = q_in.shape
    pool = n_in.shape[0]
    wide = PLANE * rows
    two = 2 * rows
    lanes = hwb.shape[2]
    chunk = wide // dims
    half = planes // 2
    part = rows // SUB
    groups = planes // PLANE
    mid = SUB // 2
    across = dims // DIM_Y

    b = lax.axis_index("blk")
    e = lax.axis_index("dim")
    z = lax.div(b, PLANE)
    yc = lax.rem(b, PLANE)
    xx, yy = lax.rem(e, across), lax.div(e, across)
    core_yc = yc + 1 - 2 * lax.rem(yc, 2)
    far_yc = lax.rem(yc + 2, PLANE)
    cross_yc = PLANE - 1 - yc

    def at_plane(step):
        return (lax.rem(z + step + planes, planes) * PLANE + yc, e)

    def at_dim(p):
        return (b, lax.rem(e + p, dims))

    def at_x(step):
        return (b, yy * across + lax.rem(xx + step + across, across))

    core = (z * PLANE + core_yc, e)
    far = (z * PLANE + far_yc, e)
    other_y = at_dim(across)
    up, down = at_plane(1), at_plane(-1)

    def take(y, size, most=32):
        return pl.ds(pl.multiple_of(y * size, most), size)

    def slot_up(s):
        return jnp.maximum(planes - 1 - 2 * s, 0)

    def slot_down(s):
        return jnp.where(s == 0, planes - 1, planes - 2 * s)

    def span(u):
        return jnp.where(lax.rem(u, 2) == 1, -lax.div(planes - 1 - u, 2), lax.div(planes - u, 2))

    mine_slot = planes - 1
    behind = [mine_slot] + [max(planes - 1 - 2 * s, 0) for s in range(1, REACH + 1)]

    own = [
        pltpu.make_async_copy(q_in, qbuf.at[take(mine_slot, rows)], loc.at[0]),
        pltpu.make_async_copy(p_in, pbuf.at[take(yc, rows)], loc.at[1]),
        pltpu.make_async_copy(n_in, nbuf.at[take(yc, pool)], loc.at[2]),
        pltpu.make_async_copy(idx_in, idxb.at[mine_slot], loc.at[3]),
    ]
    for copy in own:
        copy.start()
    barrier = pltpu.get_barrier_semaphore()
    met = [at_plane(s) for s in range(1, planes)] + [core, far]
    met += [at_dim(p) for p in range(1, dims)]
    for device in met:
        pl.semaphore_signal(barrier, inc=1, device_id=device, device_id_type=MESH)
    dnb[...] = jnp.zeros_like(dnb)
    cbuf[...] = jnp.zeros_like(cbuf)
    recva[0] = jnp.zeros((rows, feats), BF16)
    recvb[0] = jnp.zeros((rows, feats), BF16)
    recva[1, mid * part : rows] = jnp.zeros((rows - mid * part, feats), BF16)
    recvb[1, 0 : mid * part] = jnp.zeros((mid * part, feats), BF16)
    for copy in own:
        copy.wait()
    pl.semaphore_wait(barrier, len(met))

    def up_copy(s, i):
        src, dst = slot_up(s - 1), slot_up(s)
        if i == SUB:
            return remote(idxb.at[src], idxb.at[dst], us.at[s, i], ur.at[s, i], up)
        src, dst = (pl.ds(pl.multiple_of(u * rows + i * part, 32), part) for u in (src, dst))
        return remote(qbuf.at[src], qbuf.at[dst], us.at[s, i], ur.at[s, i], up)

    def down_copy(s, i):
        src, dst = slot_down(s - 1), slot_down(s)
        if i == SUB:
            return remote(idxb.at[src], idxb.at[dst], ds.at[s, i], dr.at[s, i], down)
        src, dst = (pl.ds(pl.multiple_of(u * rows + i * part, 32), part) for u in (src, dst))
        return remote(qbuf.at[src], qbuf.at[dst], ds.at[s, i], dr.at[s, i], down)

    def last_up(i):
        return half if i < mid or i == SUB else half - 1

    def last_down(i):
        return half if mid <= i < SUB else half - 1

    def plane_copy(buf, size, sends, recvs, i):
        at = take(far_yc if i == 2 else yc, size)
        return remote(buf.at[at], buf.at[at], sends.at[i], recvs.at[i], far if i == 1 else core)

    p_copy = functools.partial(plane_copy, pbuf, rows, ps, pr)
    n_copy = functools.partial(plane_copy, nbuf, pool, ns, nr)

    p_copy(1).start()
    p_copy(0).start()
    for i in [SUB, *range(SUB)]:
        up_copy(1, i).start()
        down_copy(1, i).start()
    n_copy(1).start()
    n_copy(0).start()

    def beside(values):
        total = None
        width = len(values) * rows
        lane = lax.broadcasted_iota(jnp.int32, (8, width), 1)
        for i, value in enumerate(values):
            if width > lanes:
                fill = jnp.zeros((8, width - lanes), value.dtype)
                value = jnp.concatenate([value, fill], axis=1)
            if i == 0:
                total = value
            else:
                total = jnp.where(lane >= i * rows, pltpu.roll(value, i * rows, 1), total)
        return total

    def hard_copy(u):
        return remote(hp.at[u], hrecv.at[u], hss.at[u], hsr.at[u], at_plane(span(u)))

    sub = lax.broadcasted_iota(jnp.int32, (8, two), 0)

    def scored(p):
        pair = half - 1 - p
        query = qbuf[take(pair, two)]
        ids = beside([idxb[2 * pair], idxb[2 * pair + 1]]) - z * (PLANE * pool)
        idxp[pair] = ids
        low, high = ids & 7, ids >> 3
        keys = [jnp.where(low[k : k + 1] == sub, high[k : k + 1], -1) for k in range(HARD)]

        def one(y, acc):
            scores = dot(nbuf[take(y, pool)], query, 1, 1)
            base = y * (pool // 8)
            acc = list(acc)
            for r in range(pool // 8):
                tile = scores[8 * r : 8 * r + 8]
                for k in range(HARD):
                    acc[k] = jnp.where(keys[k] == base + r, tile, acc[k])
            return tuple(acc)

        acc = lax.fori_loop(0, PLANE, one, (jnp.zeros((8, two), F32),) * HARD)
        out = jnp.zeros((8, two), F32)
        for k in range(HARD):
            out = jnp.where(sub == k, jnp.sum(acc[k], axis=0, keepdims=True), out)
        hp[2 * pair] = out[:, :lanes]
        hp[2 * pair + 1] = pltpu.roll(out, rows, 1)[:, :lanes]
        hard_copy(2 * pair).start()

        @pl.when(p > 0)
        def _():
            hard_copy(2 * pair + 1).start()

    def version(y):
        return jnp.where(y >= yc, 0, 1)

    upper, lower = pl.ds(0, chunk), pl.ds(chunk, chunk)

    def block(step):
        return lax.rem(xx + step + across, across) * two // 2

    def x_copy(h, kind):
        sems = (xs.at[h, kind], xr.at[h, kind])
        ahead_at, behind_at, opposite = block(1), block(-1), block(2)

        def rows_of(start, second):
            return st.at[h, pl.ds(pl.multiple_of(start + second * chunk, 32), chunk)]

        if kind == 0:
            return remote(rows_of(opposite, 0), relay.at[h, 0], *sems, at_x(1))
        if kind == 1:
            return remote(rows_of(opposite, 1), relay.at[h, 1], *sems, at_x(-1))
        if kind == 2:
            return remote(rows_of(ahead_at, 1), nextto.at[h, 0, lower], *sems, at_x(1))
        if kind == 3:
            return remote(rows_of(behind_at, 0), nextto.at[h, 1, upper], *sems, at_x(-1))
        if kind == 4:
            return remote(merged.at[h, 0], nextto.at[h, 0, upper], *sems, at_x(1))
        return remote(merged.at[h, 1], nextto.at[h, 1, lower], *sems, at_x(-1))

    def y_copy(h):
        return remote(ysum.at[h], yget.at[h], ls.at[h], lr.at[h], other_y)

    owner = xx
    ahead = jnp.full((8, lanes), owner, jnp.int32) >= yc

    def lse_copy(g):
        return remote(wsend.at[g], wrecv.at[g], wss.at[g], wsr.at[g], at_plane(-g))

    def window_stage(h, stage):
        if stage == 0:
            if h == 0:
                for i, g in enumerate((1, 2)):
                    for v in range(2):
                        qcat[v, i * rows : (i + 1) * rows] = qbuf[take(behind[g], rows)]
            else:
                for v, g in enumerate((0, REACH)):
                    qcat[v, two : two + rows] = qbuf[take(behind[3], rows)]
                    qcat[v, two + rows : wide] = qbuf[take(behind[g], rows)]

            def one(y):
                at = take(y, rows)
                st[h, at] = dot(pbuf[at], qcat[version(y), h * two : (h + 1) * two], 1, 1)

            loop(0, PLANE, one)
            for kind in range(4):
                x_copy(h, kind).start()
        elif stage == 1:
            for side, start in ((0, block(1)), (1, block(-1))):
                x_copy(h, side).wait_recv()
                at = pl.ds(pl.multiple_of(start + side * chunk, 32), chunk)
                merged[h, side] = st[h, at] + relay[h, side]
                x_copy(h, 4 + side).start()
        elif stage == 2:
            for kind in range(2, 6):
                x_copy(h, kind).wait_recv()
            for keep, start in ((True, yy), (False, 1 - yy)):
                inner = take(start, chunk)
                at = pl.ds(pl.multiple_of(block(0) + start * chunk, 32), chunk)
                total = st[h, at] + nextto[h, 0, inner] + nextto[h, 1, inner]
                if keep:
                    mine[h] = total
                else:
                    ysum[h] = total
            y_copy(h).start()
        else:
            y_copy(h).wait_recv()
            total = (mine[h] + yget[h]) * scale
            sc[h] = total
            top = jnp.max(total, axis=0, keepdims=True)
            lse = top + jnp.log(jnp.sum(jnp.exp(total - top), axis=0, keepdims=True))
            lse = jnp.broadcast_to(lse, (8, two))
            one, another = lse[:, :lanes], pltpu.roll(lse, rows, 1)[:, :lanes]
            if h == 0:
                wsend[1] = one
                wsend[2] = another
                lse_copy(2).start()
                lse_copy(1).start()
            else:
                wsend[3] = one
                wsend[0] = jnp.where(ahead, another, LOW)
                wsend[REACH] = jnp.where(ahead, LOW, another)
                lse_copy(REACH).start()
                lse_copy(3).start()

    first = half // 2

    def ring_step(s):
        for i in [SUB, *range(SUB)]:
            up_last, down_last = last_up(i), last_down(i)

            @pl.when(s <= up_last)
            def _():
                up_copy(s, i).wait_recv()

            @pl.when(s < up_last)
            def _():
                up_copy(s + 1, i).start()

            @pl.when(s <= down_last)
            def _():
                down_copy(s, i).wait_recv()

            @pl.when(s < down_last)
            def _():
                down_copy(s + 1, i).start()

        @pl.when(s == 1)
        def _():
            p_copy(1).wait_recv()
            p_copy(2).start()

        @pl.when(s == 2)
        def _():
            p_copy(0).wait_recv()
            p_copy(2).wait_recv()

        for stage in (3, 2, 1, 0):
            for h in range(2):
                if 2 * h + 2 + stage <= half:
                    pl.when(s == 2 * h + 2 + stage)(functools.partial(window_stage, h, stage))

        @pl.when(s == first)
        def _():
            n_copy(1).wait_recv()
            n_copy(2).start()
            n_copy(0).wait_recv()
            n_copy(2).wait_recv()

        @pl.when(s >= first)
        def _():
            low = jnp.where(s == first, 0, jnp.minimum(2 * (s - first), s - 1))
            loop(low, jnp.minimum(2 * (s - first) + 2, s), scored)

    loop(1, half + 1, ring_step)
    for stage in range(4):
        for h in range(2):
            if 2 * h + 2 + stage > half:
                window_stage(h, stage)

    parts = [wsend[0]]
    for g in range(1, REACH + 1):
        lse_copy(g).wait_recv()
        parts.append(wrecv[g])

    def joined(values):
        highest = functools.reduce(jnp.maximum, values)
        return highest + jnp.log(sum(jnp.exp(value - highest) for value in values))

    window_lse = joined(parts)
    hard_sum = hp[mine_slot]
    for u in range(planes - 2, -1, -1):
        hard_copy(u).wait_recv()
        hard_sum = hard_sum + hrecv[u]
    last = lax.broadcasted_iota(jnp.int32, (8, lanes), 0) == HARD
    msg[...] = jnp.where(last, window_lse, hard_sum)

    def sum_copy(p):
        return remote(msg, arecv.at[p], ags.at[p], agr.at[p], at_dim(p))

    for p in range(1, dims):
        sum_copy(p).start()
    values = [msg[...]]
    for p in range(1, dims):
        sum_copy(p).wait_recv()
        values.append(arecv[p])
    entries = jnp.where(last, joined(values), sum(values) * scale)
    highest = jnp.max(entries, axis=0, keepdims=True)
    log_total = highest + jnp.log(jnp.sum(jnp.exp(entries - highest), axis=0, keepdims=True))
    hard_weights = jnp.exp(entries - log_total).astype(BF16).astype(F32)
    hwb[mine_slot] = jnp.where(last, log_total, hard_weights)

    def weight_copy(u):
        device = at_plane(-span(u))
        return remote(hwb.at[mine_slot], hwb.at[u], hws.at[u], hwr.at[u], device)

    loop(0, planes - 1, lambda u: weight_copy(u).start())

    logs = [jnp.broadcast_to(hwb[mine_slot, HARD : HARD + 1], (8, lanes))]
    for g in range(1, REACH + 1):
        weight_copy(behind[g]).wait_recv()
        logs.append(jnp.broadcast_to(hwb[behind[g], HARD : HARD + 1], (8, lanes)))
    halves = [beside(logs[1:3]), beside([logs[3], jnp.where(ahead, logs[0], logs[REACH])])]
    row_at = lax.broadcasted_iota(jnp.int32, (chunk, two), 0) + yy * chunk + rows
    lane_at = lax.broadcasted_iota(jnp.int32, (chunk, two), 1)
    positive = (row_at == lane_at) & (jnp.full((chunk, two), owner, jnp.int32) == yc)
    my_tile = take(xx * DIM_Y + yy, chunk)
    wt[my_tile, 0:two] = jnp.exp(sc[0] - halves[0][0:1]).astype(BF16)
    weights = jnp.exp(sc[1] - halves[1][0:1]) - jnp.where(positive, 1.0, 0.0)
    wt[my_tile, two:wide] = weights.astype(BF16)

    def tile_copy(p):
        return remote(wt.at[my_tile], wt.at[my_tile], wts.at[p], wtr.at[p], at_dim(p))

    for p in range(1, dims):
        tile_copy(p).start()

    def graded(g):
        for i in range(PLANE):
            u = PLANE * g + i
            fresh = functools.reduce(jnp.logical_and, [u != v for v in behind])

            @pl.when(fresh)
            def _():
                weight_copy(u).wait_recv()

        ids = jnp.concatenate([idxp[2 * g], idxp[2 * g + 1]], axis=1)
        pay = beside([hwb[PLANE * g + i] for i in range(PLANE)])
        counted = lax.broadcasted_iota(jnp.int32, (8, wide), 0) < HARD
        high = ids >> 4
        high = jnp.where((high >= 0) & (high < PLANE * pool // 16), high, -1)
        low = ids & 15
        deep = lax.broadcasted_iota(jnp.int32, (16, wide), 0)
        keys, held = [], []
        for k in range(HARD):
            same = jnp.where((ids == ids[k : k + 1]) & counted, pay, 0.0)
            same = jnp.sum(same, axis=0, keepdims=True)
            held.append(jnp.broadcast_to(same, (16, wide)).astype(BF16))
            key = jnp.where(low[k : k + 1] == deep, high[k : k + 1], -1)
            keys.append(key.astype(F32).astype(BF16))

        for c in range(wide // 128):
            cut = slice(c * 128, (c + 1) * 128)
            key_cut = [key[:, cut] for key in keys]
            held_cut = [value[:, cut] for value in held]

            def one(r):
                base = jnp.full((16, 128), 8 * r, jnp.int32).astype(F32).astype(BF16)
                moved = [key - base for key in key_cut]
                for i in range(8):
                    tile = jnp.zeros((16, 128), BF16)
                    for k in range(HARD):
                        tile = jnp.where(moved[k] == jnp.bfloat16(i), held_cut[k], tile)
                    wht[pl.ds(pl.multiple_of(128 * r + 16 * i, 16), 16), cut] = tile

            loop(0, PLANE * pool // 128, one)

        query = qbuf[take(g, wide)]

        def grown(y):
            at = take(y, pool)
            dnb[at] += dot(wht[at], query, 1, 0)

        loop(0, PLANE, grown)
        cbuf[take(g, wide)] += dot(wht[...], nbuf[...], 0, 0)

    def window_grads():
        for p in range(1, dims):
            tile_copy(p).wait_recv()
        tail = wide - lanes
        near = jnp.zeros((lanes, feats), F32)
        rest = jnp.zeros((lanes, feats), F32)
        for y in range(PLANE):
            at = pl.ds(y * rows, rows)
            dpb[at] = dot(wt[at], qcat[version(y)], 1, 0)
            piece = dot(wt[at, tail:wide], pbuf[at], 0, 0)
            here = jnp.full((lanes, feats), y, jnp.int32) >= yc
            near = near + jnp.where(here, piece, 0.0)
            rest = rest + jnp.where(here, 0.0, piece)
        win[0:tail] = dot(wt[:, 0:tail], pbuf[...], 0, 0)
        win[tail:wide] = near + rest
        for g in range(1, REACH):
            cbuf[take(behind[g], rows)] += win[(g - 1) * rows : g * rows]
        cbuf[take(mine_slot, rows)] += near[lanes - rows : lanes]
        cbuf[take(behind[REACH], rows)] += rest[lanes - rows : lanes]

    def a_copy(t, i):
        at = pl.ds(i * part, part)
        sems = (as_.at[t + 1, i], ar.at[t + 1, i])
        return remote(senda.at[t, at], recva.at[t + 1, at], *sems, down)

    def b_copy(t, i):
        at = pl.ds(i * part, part)
        sems = (bs.at[t + 1, i], br.at[t + 1, i])
        return remote(sendb.at[t, at], recvb.at[t + 1, at], *sems, up)

    def first_a(i):
        return 0 if i < mid else 1

    def first_b(i):
        return 1 - first_a(i)

    def core_copy(kind):
        src, dst = ((nsend, nrecv), (psend, precv))[kind]
        return remote(src, dst, cs.at[kind], cr.at[kind], core)

    def far_copy(kind):
        src, dst = ((nfar, ngot), (pfar, pgot))[kind]
        return remote(src, dst, ys.at[kind], yr.at[kind], far)

    def core_stage(kind):
        total, size, send = ((dnb, pool, nsend), (dpb, rows, psend))[kind]
        for i, y in enumerate((core_yc, cross_yc)):
            send[i] = total[take(y, size)].astype(BF16)
        core_copy(kind).start()

    def far_stage(kind):
        total, size, got, send = ((dnb, pool, nrecv, nfar), (dpb, rows, precv, pfar))[kind]
        core_copy(kind).wait_recv()
        send[...] = (total[take(far_yc, size)] + got[1].astype(F32)).astype(BF16)
        far_copy(kind).start()

    window_at = half - REACH - 1

    def back_step(t):
        ua, ub = jnp.maximum(2 * t - 1, 0), 2 * t
        for i in range(SUB):
            for begin, u, copy, got, send in (
                (first_a(i), ua, a_copy, recva, senda),
                (first_b(i), ub, b_copy, recvb, sendb),
            ):

                @pl.when(t > begin)
                def _():
                    copy(t - 1, i).wait_recv()

                @pl.when(t >= begin)
                def _():
                    at = pl.ds(i * part, part)
                    piece = cbuf[pl.ds(pl.multiple_of(u * rows + i * part, 32), part)]
                    send[t, at] = (piece + got[t, at].astype(F32)).astype(BF16)
                    copy(t, i).start()

        @pl.when(t < groups - 1)
        def _():
            graded(t + 1)

        pl.when(t == groups - 2)(functools.partial(core_stage, 0))
        pl.when(t == groups - 1)(functools.partial(far_stage, 0))
        if window_at >= 0:

            @pl.when(t == window_at)
            def _():
                window_grads()
                core_stage(1)

        pl.when(t == max(window_at, 0) + 1)(functools.partial(far_stage, 1))

    loop(0, 1, graded)
    if window_at < 0:
        window_grads()
        core_stage(1)
    loop(0, half, back_step)

    for kind, total, size, got, crossed, out in (
        (0, dnb, pool, nrecv, ngot, dn_out),
        (1, dpb, rows, precv, pgot, dp_out),
    ):
        far_copy(kind).wait_recv()
        back = got[0].astype(F32) + crossed[...].astype(F32)
        out[...] = (total[take(yc, size)] + back) * scale
    for i in range(SUB):
        a_copy(half - 1, i).wait_recv()
        b_copy(half - 1, i).wait_recv()
    back = recva[half].astype(F32) + recvb[half].astype(F32)
    gq_out[...] = (cbuf[take(mine_slot, rows)] + back) * scale

    for i in range(SUB + 1):
        loop(1, last_up(i) + 1, lambda s: up_copy(s, i).wait_send())
        loop(1, last_down(i) + 1, lambda s: down_copy(s, i).wait_send())
    for i in range(3):
        p_copy(i).wait_send()
        n_copy(i).wait_send()
    for h in range(2):
        for kind in range(6):
            x_copy(h, kind).wait_send()
        y_copy(h).wait_send()
    for p in range(1, dims):
        sum_copy(p).wait_send()
        tile_copy(p).wait_send()
    for g in range(1, REACH + 1):
        lse_copy(g).wait_send()
    loop(0, planes - 1, lambda u: hard_copy(u).wait_send())
    loop(0, planes - 1, lambda u: weight_copy(u).wait_send())
    for i in range(SUB):
        loop(first_a(i), half, lambda t: a_copy(t, i).wait_send())
        loop(first_b(i), half, lambda t: b_copy(t, i).wait_send())
    for kind in range(2):
        core_copy(kind).wait_send()
        far_copy(kind).wait_send()


def on_device(queries, passages, negatives, hard_index):
    rows, feats = queries.shape
    pool = negatives.shape[0]
    planes = lax.axis_size("blk") // PLANE
    dims = lax.axis_size("dim")
    half = planes // 2
    wide, two = PLANE * rows, 2 * rows
    chunk = wide // dims
    lanes = -(-rows // 128) * 128
    index = jnp.pad(hard_index.T, ((0, 8 - HARD), (0, lanes - rows)), constant_values=-1)

    dma = pltpu.SemaphoreType.DMA
    vmem = pltpu.VMEM
    scratch = [
        vmem((planes * rows, feats), BF16),
        vmem((planes, 8, lanes), jnp.int32),
        vmem((half, 8, two), jnp.int32),
        vmem((wide, feats), BF16),
        vmem((PLANE * pool, feats), BF16),
        vmem((2, wide, feats), BF16),
        vmem((2, wide, two), F32),
        vmem((2, 2, chunk, two), F32),
        vmem((2, 2, chunk, two), F32),
        vmem((2, 2, 2 * chunk, two), F32),
        vmem((2, chunk, two), F32),
        vmem((2, chunk, two), F32),
        vmem((2, chunk, two), F32),
        vmem((2, chunk, two), F32),
        vmem((planes, 8, lanes), F32),
        vmem((planes, 8, lanes), F32),
        vmem((REACH + 1, 8, lanes), F32),
        vmem((REACH + 1, 8, lanes), F32),
        vmem((8, lanes), F32),
        vmem((dims, 8, lanes), F32),
        vmem((planes, 8, lanes), F32),
        vmem((wide, wide), BF16),
        vmem((PLANE * pool, wide), BF16),
        vmem((planes * rows, feats), F32),
        vmem((wide, feats), F32),
        vmem((PLANE * pool, feats), F32),
        vmem((wide, feats), F32),
        vmem((half + 1, rows, feats), BF16),
        vmem((half + 1, rows, feats), BF16),
        vmem((half, rows, feats), BF16),
        vmem((half, rows, feats), BF16),
        vmem((2, pool, feats), BF16),
        vmem((2, pool, feats), BF16),
        vmem((2, rows, feats), BF16),
        vmem((2, rows, feats), BF16),
        vmem((pool, feats), BF16),
        vmem((pool, feats), BF16),
        vmem((rows, feats), BF16),
        vmem((rows, feats), BF16),
        dma((4,)),
    ]
    for shape in (
        (half + 1, SUB + 1), (half + 1, SUB + 1), (3,), (3,), (2, 6), (2,), (planes,), (REACH + 1,),
        (dims,), (planes,), (dims,), (half + 1, SUB), (half + 1, SUB), (2,), (2,),
    ):
        scratch += [dma(shape), dma(shape)]

    return pl.pallas_call(
        functools.partial(kernel, planes, dims),
        out_shape=(
            jax.ShapeDtypeStruct((rows, feats), F32),
            jax.ShapeDtypeStruct((rows, feats), F32),
            jax.ShapeDtypeStruct((pool, feats), F32),
        ),
        in_specs=[pl.BlockSpec(memory_space=pl.ANY)] * 4,
        out_specs=[pl.BlockSpec(memory_space=pltpu.VMEM)] * 3,
        scratch_shapes=scratch,
        compiler_params=pltpu.CompilerParams(
            collective_id=0, has_side_effects=True, vmem_limit_bytes=50 * 1024 * 1024
        ),
    )(queries, passages, negatives, index)


def solution(mesh):
    placed = (P("blk", "dim"), P("blk", "dim"), P("blk", "dim"), P("blk", None))
    return jax.shard_map(
        on_device,
        mesh=mesh,
        in_specs=placed,
        out_specs=(P("blk", "dim"), P("blk", "dim"), P("blk", "dim")),
        check_vma=False,
    )
```

time: 162 us -> 146 us (0.901)
  Pallas kernels: 156 us -> 138 us
    pallas_call x1, Pallas kernels: 156 us -> 138 us  [on_device(): pl.pallas_call(functools.partial(kernel, planes, dims), out_shape=(jax.Sh...]
    unnamed x5 -> x9, local copies, waits for them, and re-layouts: 4.49 us -> 5.22 us
where the time goes in v2:
time: 146 us; the launch traced here: 145 us
  Pallas kernels  138 us (95%)
  local copies, waits for them, and re-layouts  5.92 us (4%)
    pallas_call x1, Pallas kernels, on_device(): pl.pallas_call(functools.partial(kernel, planes, dims), out_shape=(jax.Sh...  138 us
    unnamed x9, local copies, waits for them, and re-layouts  5.22 us

profile of v2, /device:TPU:1, one launch (start us, length us, event | category | flops | bytes accessed | tf_op | source)
XLA Modules:
  0.0 145.0 jit_solution(3028117237745050718)
XLA Ops:
  0.6 0.7 pad.4.idx_in
  1.3 0.0 copy-start
  1.3 1.0 copy-done
  2.3 0.0 copy-start.1
  2.3 0.9 copy-done.1
  3.3 0.0 copy-start.2
  3.3 0.9 copy-done.2
  4.2 138.5 %shard_map.67 = (f32[192,512]{1,0:T(8,128)S(1)}, f32[192,512]{1,0:T(8,128)S(1)}, f32[384,512]{1,0:T(8,128)S(1)}) custom-call(bf16[192,512]{1,0:T(8,128)(2,1)S(1)} %copy-done.1, bf16[192,512]{1,0:T(8,128)(2,1)S(1)} %copy-done.2, bf16[384,512]{1,0:T(8,128)(2,1)S(1)} %copy-done, s32[8,256]{1,0:T(8,128)S(1)} %pad.4.idx_in), custom_call_target="tpu_custom_call" | custom-call | tf_op jit(solution)/shard_map/pallas_call | solution.py:666
  142.7 0.7 copy.10
  143.4 0.7 copy.11
  144.1 0.9 copy.12
Async XLA Ops:
  1.3 1.0 copy-start
  2.3 0.9 copy-start.1
  3.3 0.9 copy-start.2

commit v3 on v2

--- a/solution.py
+++ b/solution.py
@@ -51,7 +51,7 @@
     planes, dims,
     q_in, p_in, n_in, idx_in, gq_out, dp_out, dn_out,
     qbuf, idxb, idxp, pbuf, nbuf, qcat, st, relay, merged, nextto, mine, ysum, yget, sc,
-    hp, hrecv, wsend, wrecv, msg, arecv, hwb, wt, wht, cbuf, win, dnb, dpb,
+    hpair, hp, hrecv, wsend, wrecv, msg, arecv, hwb, wt, wht, cbuf, win, dnb, dpb,
     recva, recvb, senda, sendb, nsend, nrecv, psend, precv, nfar, ngot, pfar, pgot,
     loc, us, ur, ds, dr, ps, pr, ns, nr, xs, xr, ls, lr, hss, hsr, wss, wsr, ags, agr,
     hws, hwr, wts, wtr, as_, ar, bs, br, cs, cr, ys, yr,
@@ -119,50 +119,50 @@
     met += [at_dim(p) for p in range(1, dims)]
     for device in met:
         pl.semaphore_signal(barrier, inc=1, device_id=device, device_id_type=MESH)
+    for copy in own:
+        copy.wait()
+    pl.semaphore_wait(barrier, len(met))
+
+    def up_copy(s, i):
+        src, dst = slot_up(s - 1), slot_up(s)
+        if i == SUB:
+            return remote(idxb.at[src], idxb.at[dst], us.at[s, i], ur.at[s, i], up)
+        src, dst = (pl.ds(pl.multiple_of(u * rows + i * part, 32), part) for u in (src, dst))
+        return remote(qbuf.at[src], qbuf.at[dst], us.at[s, i], ur.at[s, i], up)
+
+    def down_copy(s, i):
+        src, dst = slot_down(s - 1), slot_down(s)
+        if i == SUB:
+            return remote(idxb.at[src], idxb.at[dst], ds.at[s, i], dr.at[s, i], down)
+        src, dst = (pl.ds(pl.multiple_of(u * rows + i * part, 32), part) for u in (src, dst))
+        return remote(qbuf.at[src], qbuf.at[dst], ds.at[s, i], dr.at[s, i], down)
+
+    def last_up(i):
+        return half if i < mid or i == SUB else half - 1
+
+    def last_down(i):
+        return half if mid <= i < SUB else half - 1
+
+    def plane_copy(buf, size, sends, recvs, i):
+        at = take(far_yc if i == 2 else yc, size)
+        return remote(buf.at[at], buf.at[at], sends.at[i], recvs.at[i], far if i == 1 else core)
+
+    p_copy = functools.partial(plane_copy, pbuf, rows, ps, pr)
+    n_copy = functools.partial(plane_copy, nbuf, pool, ns, nr)
+
+    p_copy(1).start()
+    p_copy(0).start()
+    for i in [SUB, *range(SUB)]:
+        up_copy(1, i).start()
+        down_copy(1, i).start()
+    n_copy(0).start()
+    n_copy(1).start()
     dnb[...] = jnp.zeros_like(dnb)
     cbuf[...] = jnp.zeros_like(cbuf)
     recva[0] = jnp.zeros((rows, feats), BF16)
     recvb[0] = jnp.zeros((rows, feats), BF16)
     recva[1, mid * part : rows] = jnp.zeros((rows - mid * part, feats), BF16)
     recvb[1, 0 : mid * part] = jnp.zeros((mid * part, feats), BF16)
-    for copy in own:
-        copy.wait()
-    pl.semaphore_wait(barrier, len(met))
-
-    def up_copy(s, i):
-        src, dst = slot_up(s - 1), slot_up(s)
-        if i == SUB:
-            return remote(idxb.at[src], idxb.at[dst], us.at[s, i], ur.at[s, i], up)
-        src, dst = (pl.ds(pl.multiple_of(u * rows + i * part, 32), part) for u in (src, dst))
-        return remote(qbuf.at[src], qbuf.at[dst], us.at[s, i], ur.at[s, i], up)
-
-    def down_copy(s, i):
-        src, dst = slot_down(s - 1), slot_down(s)
-        if i == SUB:
-            return remote(idxb.at[src], idxb.at[dst], ds.at[s, i], dr.at[s, i], down)
-        src, dst = (pl.ds(pl.multiple_of(u * rows + i * part, 32), part) for u in (src, dst))
-        return remote(qbuf.at[src], qbuf.at[dst], ds.at[s, i], dr.at[s, i], down)
-
-    def last_up(i):
-        return half if i < mid or i == SUB else half - 1
-
-    def last_down(i):
-        return half if mid <= i < SUB else half - 1
-
-    def plane_copy(buf, size, sends, recvs, i):
-        at = take(far_yc if i == 2 else yc, size)
-        return remote(buf.at[at], buf.at[at], sends.at[i], recvs.at[i], far if i == 1 else core)
-
-    p_copy = functools.partial(plane_copy, pbuf, rows, ps, pr)
-    n_copy = functools.partial(plane_copy, nbuf, pool, ns, nr)
-
-    p_copy(1).start()
-    p_copy(0).start()
-    for i in [SUB, *range(SUB)]:
-        up_copy(1, i).start()
-        down_copy(1, i).start()
-    n_copy(1).start()
-    n_copy(0).start()
 
     def beside(values):
         total = None
@@ -181,37 +181,42 @@
     def hard_copy(u):
         return remote(hp.at[u], hrecv.at[u], hss.at[u], hsr.at[u], at_plane(span(u)))
 
-    sub = lax.broadcasted_iota(jnp.int32, (8, two), 0)
-
-    def scored(p):
+    chip = 2 * lax.div(yc, 2)
+
+    def scored(p, across_y):
         pair = half - 1 - p
         query = qbuf[take(pair, two)]
-        ids = beside([idxb[2 * pair], idxb[2 * pair + 1]]) - z * (PLANE * pool)
-        idxp[pair] = ids
-        low, high = ids & 7, ids >> 3
-        keys = [jnp.where(low[k : k + 1] == sub, high[k : k + 1], -1) for k in range(HARD)]
-
-        def one(y, acc):
-            scores = dot(nbuf[take(y, pool)], query, 1, 1)
-            base = y * (pool // 8)
-            acc = list(acc)
+        begin = jnp.where(across_y == 1, 2 - chip, chip)
+
+        @pl.when(across_y == 0)
+        def _():
+            ids = beside([idxb[2 * pair], idxb[2 * pair + 1]])
+            idxp[pair] = ids - z * (PLANE * pool)
+            hpair[pair] = jnp.zeros((8, two), F32)
+
+        low, high = idxp[pair] & 7, idxp[pair] >> 3
+
+        def one(i, acc):
+            scores = dot(nbuf[take(begin + i, pool)], query, 1, 1)
+            base = (begin + i) * (pool // 8)
             for r in range(pool // 8):
                 tile = scores[8 * r : 8 * r + 8]
-                for k in range(HARD):
-                    acc[k] = jnp.where(keys[k] == base + r, tile, acc[k])
-            return tuple(acc)
-
-        acc = lax.fori_loop(0, PLANE, one, (jnp.zeros((8, two), F32),) * HARD)
-        out = jnp.zeros((8, two), F32)
-        for k in range(HARD):
-            out = jnp.where(sub == k, jnp.sum(acc[k], axis=0, keepdims=True), out)
-        hp[2 * pair] = out[:, :lanes]
-        hp[2 * pair + 1] = pltpu.roll(out, rows, 1)[:, :lanes]
-        hard_copy(2 * pair).start()
-
-        @pl.when(p > 0)
+                picked = jnp.take_along_axis(tile, low, axis=0, mode="promise_in_bounds")
+                acc = jnp.where(high == base + r, picked, acc)
+            return acc
+
+        out = lax.fori_loop(0, 2, one, hpair[pair])
+        hpair[pair] = out
+
+        @pl.when(across_y == 1)
         def _():
-            hard_copy(2 * pair + 1).start()
+            hp[2 * pair] = out[:, :lanes]
+            hp[2 * pair + 1] = pltpu.roll(out, rows, 1)[:, :lanes]
+            hard_copy(2 * pair).start()
+
+            @pl.when(p > 0)
+            def _():
+                hard_copy(2 * pair + 1).start()
 
     def version(y):
         return jnp.where(y >= yc, 0, 1)
@@ -306,6 +311,28 @@
                 lse_copy(3).start()
 
     first = half // 2
+    jobs, left = [], list(range(half))
+    for s in range(1, half + 1):
+        early = 0 if s < first else 2 if s == half else 1
+        jobs.append([(left.pop(0), 1) for _ in range(early) if left and left[0] <= s - 2])
+        jobs.append([(s - 1, 0)])
+        if s == first:
+            jobs[-1] += [(left.pop(0), 1)]
+    jobs[-1] += [(p, 1) for p in left]
+    queue = sum(jobs, [])
+
+    def lookup(index, values):
+        found = jnp.int32(values[0])
+        for i, value in enumerate(values):
+            found = jnp.where(index >= i, value, found)
+        return found
+
+    ends = [sum(len(some) for some in jobs[: i + 1]) for i in range(len(jobs))]
+
+    def queued(q):
+        scored(lookup(q, [p for p, _ in queue]), lookup(q, [kind for _, kind in queue]))
+
+    stage_at = {0: 0, 1: 1, 2: 3, 3: 4}
 
     def ring_step(s):
         for i in [SUB, *range(SUB)]:
@@ -326,38 +353,46 @@
             @pl.when(s < down_last)
             def _():
                 down_copy(s + 1, i).start()
+
+            if i == SUB:
+                continue
+            if i == 0:
+
+                @pl.when(s == 1)
+                def _():
+                    n_copy(0).wait_recv()
+
+                @pl.when(s == 2)
+                def _():
+                    p_copy(0).wait_recv()
+                    p_copy(2).wait_recv()
+
+                @pl.when(s == first)
+                def _():
+                    n_copy(1).wait_recv()
+                    n_copy(2).start()
+                    n_copy(2).wait_recv()
+
+            if i < 2:
+                slot = 2 * (s - 1) + i
+                low = jnp.where(slot == 0, 0, lookup(slot - 1, ends))
+                loop(low, lookup(slot, ends), queued)
 
         @pl.when(s == 1)
         def _():
             p_copy(1).wait_recv()
             p_copy(2).start()
 
-        @pl.when(s == 2)
-        def _():
-            p_copy(0).wait_recv()
-            p_copy(2).wait_recv()
-
         for stage in (3, 2, 1, 0):
             for h in range(2):
-                if 2 * h + 2 + stage <= half:
-                    pl.when(s == 2 * h + 2 + stage)(functools.partial(window_stage, h, stage))
-
-        @pl.when(s == first)
-        def _():
-            n_copy(1).wait_recv()
-            n_copy(2).start()
-            n_copy(0).wait_recv()
-            n_copy(2).wait_recv()
-
-        @pl.when(s >= first)
-        def _():
-            low = jnp.where(s == first, 0, jnp.minimum(2 * (s - first), s - 1))
-            loop(low, jnp.minimum(2 * (s - first) + 2, s), scored)
+                step = 2 * h + 2 + stage_at[stage]
+                if step <= half:
+                    pl.when(s == step)(functools.partial(window_stage, h, stage))
 
     loop(1, half + 1, ring_step)
     for stage in range(4):
         for h in range(2):
-            if 2 * h + 2 + stage > half:
+            if 2 * h + 2 + stage_at[stage] > half:
                 window_stage(h, stage)
 
     parts = [wsend[0]]
@@ -457,13 +492,14 @@
 
             loop(0, PLANE * pool // 128, one)
 
+    def grown(g):
         query = qbuf[take(g, wide)]
 
-        def grown(y):
+        def one(y):
             at = take(y, pool)
             dnb[at] += dot(wht[at], query, 1, 0)
 
-        loop(0, PLANE, grown)
+        loop(0, PLANE, one)
         cbuf[take(g, wide)] += dot(wht[...], nbuf[...], 0, 0)
 
     def window_grads():
@@ -543,9 +579,8 @@
                     send[t, at] = (piece + got[t, at].astype(F32)).astype(BF16)
                     copy(t, i).start()
 
-        @pl.when(t < groups - 1)
-        def _():
-            graded(t + 1)
+            if i < 2:
+                pl.when(t < groups - 1)(functools.partial((graded, grown)[i], t + 1))
 
         pl.when(t == groups - 2)(functools.partial(core_stage, 0))
         pl.when(t == groups - 1)(functools.partial(far_stage, 0))
@@ -559,6 +594,7 @@
         pl.when(t == max(window_at, 0) + 1)(functools.partial(far_stage, 1))
 
     loop(0, 1, graded)
+    loop(0, 1, grown)
     if window_at < 0:
         window_grads()
         core_stage(1)
@@ -630,6 +666,7 @@
         vmem((2, chunk, two), F32),
         vmem((2, chunk, two), F32),
         vmem((2, chunk, two), F32),
+        vmem((half, 8, two), F32),
         vmem((planes, 8, lanes), F32),
         vmem((planes, 8, lanes), F32),
         vmem((REACH + 1, 8, lanes), F32),

time: 146 us -> 137 us (0.938)
  Pallas kernels: 138 us -> 129 us
    pallas_call x1, Pallas kernels: 138 us -> 129 us  [on_device(): pl.pallas_call(functools.partial(kernel, planes, dims), out_shape=(jax.Sh...]
where the time goes in v3:
time: 137 us; the launch traced here: 135 us
  Pallas kernels  129 us (94%)
  local copies, waits for them, and re-layouts  5.92 us (4%)
    pallas_call x1, Pallas kernels, on_device(): pl.pallas_call(functools.partial(kernel, planes, dims), out_shape=(jax.Sh...  129 us
    unnamed x9, local copies, waits for them, and re-layouts  5.22 us

profile of v3, /device:TPU:1, one launch (start us, length us, event | category | flops | bytes accessed | tf_op | source)
XLA Modules:
  0.0 135.1 jit_solution(105635436740469170)
XLA Ops:
  0.6 0.7 pad.4.idx_in
  1.3 0.0 copy-start
  1.3 1.0 copy-done
  2.3 0.0 copy-start.1
  2.3 0.9 copy-done.1
  3.3 0.0 copy-start.2
  3.3 0.9 copy-done.2
  4.2 128.5 %shard_map.67 = (f32[192,512]{1,0:T(8,128)S(1)}, f32[192,512]{1,0:T(8,128)S(1)}, f32[384,512]{1,0:T(8,128)S(1)}) custom-call(bf16[192,512]{1,0:T(8,128)(2,1)S(1)} %copy-done.1, bf16[192,512]{1,0:T(8,128)(2,1)S(1)} %copy-done.2, bf16[384,512]{1,0:T(8,128)(2,1)S(1)} %copy-done, s32[8,256]{1,0:T(8,128)S(1)} %pad.4.idx_in), custom_call_target="tpu_custom_call" | custom-call | tf_op jit(solution)/shard_map/pallas_call | solution.py:703
  132.7 0.7 copy.10
  133.5 0.7 copy.11
  134.2 0.9 copy.12
Async XLA Ops:
  1.3 1.0 copy-start
  2.3 0.9 copy-start.1
  3.3 0.9 copy-start.2

commit v4 on v3

--- a/solution.py
+++ b/solution.py
@@ -50,17 +50,17 @@
 def kernel(
     planes, dims,
     q_in, p_in, n_in, idx_in, gq_out, dp_out, dn_out,
-    qbuf, idxb, idxp, pbuf, nbuf, qcat, st, relay, merged, nextto, mine, ysum, yget, sc,
-    hpair, hp, hrecv, wsend, wrecv, msg, arecv, hwb, wt, wht, cbuf, win, dnb, dpb,
+    qbuf, idx0, idxb, idxp, pbuf, nbuf, qcat, st, relay, merged, nextto, mine, ysum, yget, sc,
+    hpair, hp, hrecv, wsend, wrecv, msg, arecv, hwb, logb, wt, keyb, heldb, wht, cbuf, win, dnb, dpb,
     recva, recvb, senda, sendb, nsend, nrecv, psend, precv, nfar, ngot, pfar, pgot,
     loc, us, ur, ds, dr, ps, pr, ns, nr, xs, xr, ls, lr, hss, hsr, wss, wsr, ags, agr,
-    hws, hwr, wts, wtr, as_, ar, bs, br, cs, cr, ys, yr,
+    hws, hwr, los, lor, wts, wtr, as_, ar, bs, br, cs, cr, ys, yr,
 ):
     rows, feats = q_in.shape
     pool = n_in.shape[0]
     wide = PLANE * rows
     two = 2 * rows
-    lanes = hwb.shape[2]
+    lanes = logb.shape[2]
     chunk = wide // dims
     half = planes // 2
     part = rows // SUB
@@ -110,7 +110,7 @@
         pltpu.make_async_copy(q_in, qbuf.at[take(mine_slot, rows)], loc.at[0]),
         pltpu.make_async_copy(p_in, pbuf.at[take(yc, rows)], loc.at[1]),
         pltpu.make_async_copy(n_in, nbuf.at[take(yc, pool)], loc.at[2]),
-        pltpu.make_async_copy(idx_in, idxb.at[mine_slot], loc.at[3]),
+        pltpu.make_async_copy(idx_in, idx0, loc.at[3]),
     ]
     for copy in own:
         copy.start()
@@ -121,27 +121,35 @@
         pl.semaphore_signal(barrier, inc=1, device_id=device, device_id_type=MESH)
     for copy in own:
         copy.wait()
+    idxb[mine_slot] = jnp.full((8, lanes), -1, jnp.int32)
+    idxb[mine_slot, 0:HARD, 0:rows] = idx0[...]
     pl.semaphore_wait(barrier, len(met))
+
+    def first_a(i):
+        return jnp.where(i < mid, 0, 1) if isinstance(i, jax.Array) else int(i >= mid)
+
+    def first_b(i):
+        return 1 - first_a(i)
 
     def up_copy(s, i):
         src, dst = slot_up(s - 1), slot_up(s)
-        if i == SUB:
+        if i is SUB:
             return remote(idxb.at[src], idxb.at[dst], us.at[s, i], ur.at[s, i], up)
-        src, dst = (pl.ds(pl.multiple_of(u * rows + i * part, 32), part) for u in (src, dst))
+        src, dst = (pl.ds(pl.multiple_of(u * rows + i * part, 16), part) for u in (src, dst))
         return remote(qbuf.at[src], qbuf.at[dst], us.at[s, i], ur.at[s, i], up)
 
     def down_copy(s, i):
         src, dst = slot_down(s - 1), slot_down(s)
-        if i == SUB:
+        if i is SUB:
             return remote(idxb.at[src], idxb.at[dst], ds.at[s, i], dr.at[s, i], down)
-        src, dst = (pl.ds(pl.multiple_of(u * rows + i * part, 32), part) for u in (src, dst))
+        src, dst = (pl.ds(pl.multiple_of(u * rows + i * part, 16), part) for u in (src, dst))
         return remote(qbuf.at[src], qbuf.at[dst], ds.at[s, i], dr.at[s, i], down)
 
     def last_up(i):
-        return half if i < mid or i == SUB else half - 1
+        return half if i is SUB else half - 1 + first_b(i)
 
     def last_down(i):
-        return half if mid <= i < SUB else half - 1
+        return half - 1 if i is SUB else half - 1 + first_a(i)
 
     def plane_copy(buf, size, sends, recvs, i):
         at = take(far_yc if i == 2 else yc, size)
@@ -156,8 +164,6 @@
         up_copy(1, i).start()
         down_copy(1, i).start()
     n_copy(0).start()
-    n_copy(1).start()
-    dnb[...] = jnp.zeros_like(dnb)
     cbuf[...] = jnp.zeros_like(cbuf)
     recva[0] = jnp.zeros((rows, feats), BF16)
     recvb[0] = jnp.zeros((rows, feats), BF16)
@@ -270,7 +276,7 @@
                 st[h, at] = dot(pbuf[at], qcat[version(y), h * two : (h + 1) * two], 1, 1)
 
             loop(0, PLANE, one)
-            for kind in range(4):
+            for kind in range(2):
                 x_copy(h, kind).start()
         elif stage == 1:
             for side, start in ((0, block(1)), (1, block(-1))):
@@ -278,6 +284,8 @@
                 at = pl.ds(pl.multiple_of(start + side * chunk, 32), chunk)
                 merged[h, side] = st[h, at] + relay[h, side]
                 x_copy(h, 4 + side).start()
+            for kind in (2, 3):
+                x_copy(h, kind).start()
         elif stage == 2:
             for kind in range(2, 6):
                 x_copy(h, kind).wait_recv()
@@ -332,73 +340,81 @@
     def queued(q):
         scored(lookup(q, [p for p, _ in queue]), lookup(q, [kind for _, kind in queue]))
 
-    stage_at = {0: 0, 1: 1, 2: 3, 3: 4}
-
-    def ring_step(s):
-        for i in [SUB, *range(SUB)]:
-            up_last, down_last = last_up(i), last_down(i)
-
-            @pl.when(s <= up_last)
-            def _():
-                up_copy(s, i).wait_recv()
-
-            @pl.when(s < up_last)
-            def _():
-                up_copy(s + 1, i).start()
-
-            @pl.when(s <= down_last)
-            def _():
-                down_copy(s, i).wait_recv()
-
-            @pl.when(s < down_last)
-            def _():
-                down_copy(s + 1, i).start()
-
-            if i == SUB:
-                continue
-            if i == 0:
-
-                @pl.when(s == 1)
-                def _():
-                    n_copy(0).wait_recv()
-
-                @pl.when(s == 2)
-                def _():
-                    p_copy(0).wait_recv()
-                    p_copy(2).wait_recv()
-
-                @pl.when(s == first)
-                def _():
-                    n_copy(1).wait_recv()
-                    n_copy(2).start()
-                    n_copy(2).wait_recv()
-
-            if i < 2:
-                slot = 2 * (s - 1) + i
-                low = jnp.where(slot == 0, 0, lookup(slot - 1, ends))
-                loop(low, lookup(slot, ends), queued)
-
-        @pl.when(s == 1)
+    stage_at = {(0, 0): 3, (0, 1): 5, (0, 2): 9, (0, 3): 12, (1, 0): 7, (1, 1): 10, (1, 2): 14}
+
+    def ring_move(s, i):
+        up_last, down_last = last_up(i), last_down(i)
+
+        @pl.when(s <= up_last)
+        def _():
+            up_copy(s, i).wait_recv()
+
+        @pl.when(s < up_last)
+        def _():
+            up_copy(s + 1, i).start()
+
+        @pl.when(s <= down_last)
+        def _():
+            down_copy(s, i).wait_recv()
+
+        @pl.when(s < down_last)
+        def _():
+            down_copy(s + 1, i).start()
+
+    def ring_slot(slot):
+        s, i = lax.div(slot, SUB) + 1, lax.rem(slot, SUB)
+
+        @pl.when(i == 0)
+        def _():
+            ring_move(s, SUB)
+
+        ring_move(s, i)
+
+        @pl.when(slot == 0)
+        def _():
+            n_copy(0).wait_recv()
+
+        @pl.when(slot == 1)
         def _():
             p_copy(1).wait_recv()
             p_copy(2).start()
-
-        for stage in (3, 2, 1, 0):
-            for h in range(2):
-                step = 2 * h + 2 + stage_at[stage]
-                if step <= half:
-                    pl.when(s == step)(functools.partial(window_stage, h, stage))
-
-    loop(1, half + 1, ring_step)
-    for stage in range(4):
-        for h in range(2):
-            if 2 * h + 2 + stage_at[stage] > half:
-                window_stage(h, stage)
+            n_copy(1).start()
+
+        @pl.when(slot == 2)
+        def _():
+            p_copy(0).wait_recv()
+            p_copy(2).wait_recv()
+
+        @pl.when(slot == 2 * (first - 1))
+        def _():
+            n_copy(1).wait_recv()
+            n_copy(2).start()
+            n_copy(2).wait_recv()
+
+        for (h, stage), when in stage_at.items():
+            if stage > 0:
+                pl.when(slot == when)(functools.partial(window_stage, h, stage))
+        low = jnp.where(slot == 0, 0, lookup(slot - 1, ends))
+        loop(low, lookup(slot, ends), queued)
+        for (h, stage), when in stage_at.items():
+            if stage == 0:
+                pl.when(slot == when)(functools.partial(window_stage, h, stage))
+
+    loop(0, SUB * half, ring_slot)
+    window_stage(1, 3)
 
     parts = [wsend[0]]
     for g in range(1, REACH + 1):
         lse_copy(g).wait_recv()
         parts.append(wrecv[g])
+
+    def folded(value):
+        cuts = [value[:, c : c + 128] for c in range(0, lanes, 128)]
+        return jnp.concatenate(cuts, axis=0).astype(BF16)
+
+    def unfolded(value):
+        value = value.astype(F32)
+        return jnp.concatenate([value[c : c + 8] for c in range(0, lanes // 16, 8)], axis=1)
 
     def joined(values):
         highest = functools.reduce(jnp.maximum, values)
@@ -424,19 +440,26 @@
     entries = jnp.where(last, joined(values), sum(values) * scale)
     highest = jnp.max(entries, axis=0, keepdims=True)
     log_total = highest + jnp.log(jnp.sum(jnp.exp(entries - highest), axis=0, keepdims=True))
-    hard_weights = jnp.exp(entries - log_total).astype(BF16).astype(F32)
-    hwb[mine_slot] = jnp.where(last, log_total, hard_weights)
+    hard_weights = jnp.exp(entries - log_total)
+    hwb[mine_slot] = folded(hard_weights)
+    logb[0] = jnp.broadcast_to(log_total, (8, lanes))
+
+    def log_copy(g):
+        return remote(logb.at[0], logb.at[g], los.at[g], lor.at[g], at_plane(g))
 
     def weight_copy(u):
         device = at_plane(-span(u))
         return remote(hwb.at[mine_slot], hwb.at[u], hws.at[u], hwr.at[u], device)
 
-    loop(0, planes - 1, lambda u: weight_copy(u).start())
-
-    logs = [jnp.broadcast_to(hwb[mine_slot, HARD : HARD + 1], (8, lanes))]
+    loop(0, 4, lambda u: weight_copy(u).start())
     for g in range(1, REACH + 1):
-        weight_copy(behind[g]).wait_recv()
-        logs.append(jnp.broadcast_to(hwb[behind[g], HARD : HARD + 1], (8, lanes)))
+        log_copy(g).start()
+    loop(4, planes - 1, lambda u: weight_copy(u).start())
+
+    logs = [logb[0]]
+    for g in range(1, REACH + 1):
+        log_copy(g).wait_recv()
+        logs.append(logb[g])
     halves = [beside(logs[1:3]), beside([logs[3], jnp.where(ahead, logs[0], logs[REACH])])]
     row_at = lax.broadcasted_iota(jnp.int32, (chunk, two), 0) + yy * chunk + rows
     lane_at = lax.broadcasted_iota(jnp.int32, (chunk, two), 1)
@@ -455,14 +478,13 @@
     def graded(g):
         for i in range(PLANE):
             u = PLANE * g + i
-            fresh = functools.reduce(jnp.logical_and, [u != v for v in behind])
-
-            @pl.when(fresh)
+
+            @pl.when(u != mine_slot)
             def _():
                 weight_copy(u).wait_recv()
 
         ids = jnp.concatenate([idxp[2 * g], idxp[2 * g + 1]], axis=1)
-        pay = beside([hwb[PLANE * g + i] for i in range(PLANE)])
+        pay = beside([unfolded(hwb[PLANE * g + i]) for i in range(PLANE)])
         counted = lax.broadcasted_iota(jnp.int32, (8, wide), 0) < HARD
         high = ids >> 4
         high = jnp.where((high >= 0) & (high < PLANE * pool // 16), high, -1)
@@ -476,10 +498,16 @@
             key = jnp.where(low[k : k + 1] == deep, high[k : k + 1], -1)
             keys.append(key.astype(F32).astype(BF16))
 
-        for c in range(wide // 128):
-            cut = slice(c * 128, (c + 1) * 128)
-            key_cut = [key[:, cut] for key in keys]
-            held_cut = [value[:, cut] for value in held]
+        for k in range(HARD):
+            keyb[k] = keys[k]
+            heldb[k] = held[k]
+
+    def built(g):
+        def cut_at(c):
+            cut = pl.ds(pl.multiple_of(c * 128, 128), 128)
+            out = pl.ds(pl.multiple_of(g * wide + c * 128, 128), 128)
+            key_cut = [keyb[k, :, cut] for k in range(HARD)]
+            held_cut = [heldb[k, :, cut] for k in range(HARD)]
 
             def one(r):
                 base = jnp.full((16, 128), 8 * r, jnp.int32).astype(F32).astype(BF16)
@@ -488,55 +516,59 @@
                     tile = jnp.zeros((16, 128), BF16)
                     for k in range(HARD):
                         tile = jnp.where(moved[k] == jnp.bfloat16(i), held_cut[k], tile)
-                    wht[pl.ds(pl.multiple_of(128 * r + 16 * i, 16), 16), cut] = tile
+                    wht[pl.ds(pl.multiple_of(128 * r + 16 * i, 16), 16), out] = tile
 
             loop(0, PLANE * pool // 128, one)
 
-    def grown(g):
-        query = qbuf[take(g, wide)]
-
+        loop(0, wide // 128, cut_at)
+
+    def grown(y):
+        at = take(y, pool)
+        dnb[at] = dot(wht[at], qbuf[...], 1, 0)
+
+    def returned(g):
+        at = pl.ds(pl.multiple_of(g * wide, 128), wide)
+        cbuf[take(g, wide)] += dot(wht[:, at], nbuf[...], 0, 0)
+
+    def window_documents():
         def one(y):
-            at = take(y, pool)
-            dnb[at] += dot(wht[at], query, 1, 0)
+            at = take(y, rows)
+            dpb[at] = dot(wt[at], qcat[version(y)], 1, 0)
 
         loop(0, PLANE, one)
-        cbuf[take(g, wide)] += dot(wht[...], nbuf[...], 0, 0)
-
-    def window_grads():
+
+    tail = wide - lanes
+
+    def window_queries():
         for p in range(1, dims):
             tile_copy(p).wait_recv()
-        tail = wide - lanes
+        win[0:tail] = dot(wt[:, 0:tail], pbuf[...], 0, 0)
+        for g in range(1, REACH - 1):
+            cbuf[take(behind[g], rows)] += win[(g - 1) * rows : g * rows]
+
+    def window_ends():
         near = jnp.zeros((lanes, feats), F32)
         rest = jnp.zeros((lanes, feats), F32)
         for y in range(PLANE):
             at = pl.ds(y * rows, rows)
-            dpb[at] = dot(wt[at], qcat[version(y)], 1, 0)
             piece = dot(wt[at, tail:wide], pbuf[at], 0, 0)
             here = jnp.full((lanes, feats), y, jnp.int32) >= yc
             near = near + jnp.where(here, piece, 0.0)
             rest = rest + jnp.where(here, 0.0, piece)
-        win[0:tail] = dot(wt[:, 0:tail], pbuf[...], 0, 0)
         win[tail:wide] = near + rest
-        for g in range(1, REACH):
-            cbuf[take(behind[g], rows)] += win[(g - 1) * rows : g * rows]
+        cbuf[take(behind[3], rows)] += win[two:two + rows]
         cbuf[take(mine_slot, rows)] += near[lanes - rows : lanes]
         cbuf[take(behind[REACH], rows)] += rest[lanes - rows : lanes]
 
     def a_copy(t, i):
-        at = pl.ds(i * part, part)
+        at = pl.ds(pl.multiple_of(i * part, 16), part)
         sems = (as_.at[t + 1, i], ar.at[t + 1, i])
         return remote(senda.at[t, at], recva.at[t + 1, at], *sems, down)
 
     def b_copy(t, i):
-        at = pl.ds(i * part, part)
+        at = pl.ds(pl.multiple_of(i * part, 16), part)
         sems = (bs.at[t + 1, i], br.at[t + 1, i])
         return remote(sendb.at[t, at], recvb.at[t + 1, at], *sems, up)
-
-    def first_a(i):
-        return 0 if i < mid else 1
-
-    def first_b(i):
-        return 1 - first_a(i)
 
     def core_copy(kind):
         src, dst = ((nsend, nrecv), (psend, precv))[kind]
@@ -558,14 +590,13 @@
         send[...] = (total[take(far_yc, size)] + got[1].astype(F32)).astype(BF16)
         far_copy(kind).start()
 
-    window_at = half - REACH - 1
-
-    def back_step(t):
-        ua, ub = jnp.maximum(2 * t - 1, 0), 2 * t
-        for i in range(SUB):
+    def back_slot(slot):
+        @pl.when(slot >= 1)
+        def _():
+            t, i = lax.div(slot - 1, SUB), lax.rem(slot - 1, SUB)
             for begin, u, copy, got, send in (
-                (first_a(i), ua, a_copy, recva, senda),
-                (first_b(i), ub, b_copy, recvb, sendb),
+                (first_a(i), jnp.maximum(2 * t - 1, 0), a_copy, recva, senda),
+                (first_b(i), 2 * t, b_copy, recvb, sendb),
             ):
 
                 @pl.when(t > begin)
@@ -574,31 +605,41 @@
 
                 @pl.when(t >= begin)
                 def _():
-                    at = pl.ds(i * part, part)
-                    piece = cbuf[pl.ds(pl.multiple_of(u * rows + i * part, 32), part)]
+                    at = pl.ds(pl.multiple_of(i * part, 16), part)
+                    piece = cbuf[pl.ds(pl.multiple_of(u * rows + i * part, 16), part)]
                     send[t, at] = (piece + got[t, at].astype(F32)).astype(BF16)
                     copy(t, i).start()
 
-            if i < 2:
-                pl.when(t < groups - 1)(functools.partial((graded, grown)[i], t + 1))
-
-        pl.when(t == groups - 2)(functools.partial(core_stage, 0))
-        pl.when(t == groups - 1)(functools.partial(far_stage, 0))
-        if window_at >= 0:
-
-            @pl.when(t == window_at)
-            def _():
-                window_grads()
-                core_stage(1)
-
-        pl.when(t == max(window_at, 0) + 1)(functools.partial(far_stage, 1))
-
-    loop(0, 1, graded)
-    loop(0, 1, grown)
-    if window_at < 0:
-        window_grads()
-        core_stage(1)
-    loop(0, half, back_step)
+        @pl.when(slot < groups)
+        def _():
+            graded(slot)
+            built(slot)
+
+        @pl.when((slot == 0) | (slot == 4) | (slot == 7) | (slot == 10))
+        def _():
+            returned(lax.div(slot, 3))
+
+        @pl.when((slot == 5) | (slot == 6))
+        def _():
+            grown(jnp.where(slot == 5, core_yc, far_yc))
+            grown(jnp.where(slot == 5, cross_yc, yc))
+
+        pl.when(slot == 5)(functools.partial(core_stage, 0))
+        pl.when(slot == 7)(functools.partial(far_stage, 0))
+
+        @pl.when(slot == 8)
+        def _():
+            window_queries()
+            window_ends()
+
+        @pl.when(slot == 9)
+        def _():
+            window_documents()
+            core_stage(1)
+
+        pl.when(slot == 11)(functools.partial(far_stage, 1))
+
+    loop(0, SUB * half + 1, back_slot)
 
     for kind, total, size, got, crossed, out in (
         (0, dnb, pool, nrecv, ngot, dn_out),
@@ -606,12 +647,12 @@
     ):
         far_copy(kind).wait_recv()
         back = got[0].astype(F32) + crossed[...].astype(F32)
-        out[...] = (total[take(yc, size)] + back) * scale
+        out[...] = total[take(yc, size)] + back
     for i in range(SUB):
         a_copy(half - 1, i).wait_recv()
         b_copy(half - 1, i).wait_recv()
     back = recva[half].astype(F32) + recvb[half].astype(F32)
-    gq_out[...] = (cbuf[take(mine_slot, rows)] + back) * scale
+    gq_out[...] = cbuf[take(mine_slot, rows)] + back
 
     for i in range(SUB + 1):
         loop(1, last_up(i) + 1, lambda s: up_copy(s, i).wait_send())
@@ -628,10 +669,11 @@
         tile_copy(p).wait_send()
     for g in range(1, REACH + 1):
         lse_copy(g).wait_send()
+        log_copy(g).wait_send()
     loop(0, planes - 1, lambda u: hard_copy(u).wait_send())
     loop(0, planes - 1, lambda u: weight_copy(u).wait_send())
     for i in range(SUB):
-        loop(first_a(i), half, lambda t: a_copy(t, i).wait_send())
+        loop(first_a(i), half, functools.partial(lambda i, t: a_copy(t, i).wait_send(), i))
         loop(first_b(i), half, lambda t: b_copy(t, i).wait_send())
     for kind in range(2):
         core_copy(kind).wait_send()
@@ -647,12 +689,12 @@
     wide, two = PLANE * rows, 2 * rows
     chunk = wide // dims
     lanes = -(-rows // 128) * 128
-    index = jnp.pad(hard_index.T, ((0, 8 - HARD), (0, lanes - rows)), constant_values=-1)
 
     dma = pltpu.SemaphoreType.DMA
     vmem = pltpu.VMEM
     scratch = [
         vmem((planes * rows, feats), BF16),
+        vmem((HARD, rows), jnp.int32),
         vmem((planes, 8, lanes), jnp.int32),
         vmem((half, 8, two), jnp.int32),
         vmem((wide, feats), BF16),
@@ -673,9 +715,12 @@
         vmem((REACH + 1, 8, lanes), F32),
         vmem((8, lanes), F32),
         vmem((dims, 8, lanes), F32),
-        vmem((planes, 8, lanes), F32),
+        vmem((planes, lanes // 16, 128), BF16),
+        vmem((REACH + 1, 8, lanes), F32),
         vmem((wide, wide), BF16),
-        vmem((PLANE * pool, wide), BF16),
+        vmem((HARD, 16, wide), BF16),
+        vmem((HARD, 16, wide), BF16),
+        vmem((PLANE * pool, planes * rows), BF16),
         vmem((planes * rows, feats), F32),
         vmem((wide, feats), F32),
         vmem((PLANE * pool, feats), F32),
@@ -696,24 +741,25 @@
     ]
     for shape in (
         (half + 1, SUB + 1), (half + 1, SUB + 1), (3,), (3,), (2, 6), (2,), (planes,), (REACH + 1,),
-        (dims,), (planes,), (dims,), (half + 1, SUB), (half + 1, SUB), (2,), (2,),
+        (dims,), (planes,), (REACH + 1,), (dims,), (half + 1, SUB), (half + 1, SUB), (2,), (2,),
     ):
         scratch += [dma(shape), dma(shape)]
 
-    return pl.pallas_call(
+    sums = pl.pallas_call(
         functools.partial(kernel, planes, dims),
         out_shape=(
             jax.ShapeDtypeStruct((rows, feats), F32),
             jax.ShapeDtypeStruct((rows, feats), F32),
             jax.ShapeDtypeStruct((pool, feats), F32),
         ),
-        in_specs=[pl.BlockSpec(memory_space=pl.ANY)] * 4,
+        in_specs=[pl.BlockSpec(memory_space=pltpu.HBM)] * 4,
         out_specs=[pl.BlockSpec(memory_space=pltpu.VMEM)] * 3,
         scratch_shapes=scratch,
         compiler_params=pltpu.CompilerParams(
-            collective_id=0, has_side_effects=True, vmem_limit_bytes=50 * 1024 * 1024
+            collective_id=0, has_side_effects=True, vmem_limit_bytes=60 * 1024 * 1024
         ),
-    )(queries, passages, negatives, index)
+    )(queries, passages, negatives, hard_index.T)
+    return tuple(total * scale for total in sums)
 
 
 def solution(mesh):

time: 137 us -> 134 us (0.978)
  the two profiles are of different devices: /device:TPU:1 before, /device:TPU:4 now
where the time goes in v4:
time: 134 us
  Pallas kernels  130 us (97%)
  other arithmetic  3.08 us (2%)
    pallas_call x1, Pallas kernels, on_device(): pl.pallas_call(functools.partial(kernel, planes, dims), out_shape=(jax.Sh...  130 us
    mul x2, other arithmetic, on_device(): return tuple((total * scale for total in sums))  3.08 us

profile of v4, /device:TPU:4, one launch (start us, length us, event | category | flops | bytes accessed | tf_op | source)
XLA Modules:
  0.0 134.1 jit_solution(16475361524852999735)
XLA Ops:
  0.6 130.4 %shard_map.67 = (f32[192,512]{1,0:T(8,128)}, f32[192,512]{1,0:T(8,128)}, f32[384,512]{1,0:T(8,128)}) custom-call(bf16[192,512]{1,0:T(8,128)(2,1)} %q_in.1, bf16[192,512]{1,0:T(8,128)(2,1)} %p_in.1, bf16[384,512]{1,0:T(8,128)(2,1)} %n_in.1, s32[7,192]{1,0:T(8,128)} %bitcast.1), custom_call_target="tpu_custom_call" | custom-call | tf_op jit(solution)/shard_map/pallas_call | solution.py:748
  131.0 0.0 copy-start
  131.0 2.1 %broadcast_multiply_fusion.1 = (f32[192,512]{1,0:T(8,128)}, f32[192,512]{1,0:T(8,128)}) fusion(f32[192,512]{1,0:T(8,128)} %get-tuple-element.7, f32[192,512]{1,0:T(8,128)} %get-tuple-element.6), kind=kLoop, calls=%fused_computation.1 | loop fusion | flops 196608 | bytes 1572864 | tf_op jit(solution)/shard_map/mul | solution.py:762
  133.2 0.0 copy-done
  133.2 0.9 broadcast_multiply_fusion
Async XLA Ops:
  131.0 2.1 %copy-start = (f32[384,512]{1,0:T(8,128)S(1)}, f32[384,512]{1,0:T(8,128)}, u32[]{:S(2)}) copy-start(f32[384,512]{1,0:T(8,128)} %get-tuple-element.8) | copy-start | bytes 2359300

commit v5 on v4

--- a/solution.py
+++ b/solution.py
@@ -112,13 +112,13 @@
         pltpu.make_async_copy(n_in, nbuf.at[take(yc, pool)], loc.at[2]),
         pltpu.make_async_copy(idx_in, idx0, loc.at[3]),
     ]
-    for copy in own:
-        copy.start()
     barrier = pltpu.get_barrier_semaphore()
     met = [at_plane(s) for s in range(1, planes)] + [core, far]
     met += [at_dim(p) for p in range(1, dims)]
     for device in met:
         pl.semaphore_signal(barrier, inc=1, device_id=device, device_id_type=MESH)
+    for copy in own:
+        copy.start()
     for copy in own:
         copy.wait()
     idxb[mine_slot] = jnp.full((8, lanes), -1, jnp.int32)
@@ -340,7 +340,7 @@
     def queued(q):
         scored(lookup(q, [p for p, _ in queue]), lookup(q, [kind for _, kind in queue]))
 
-    stage_at = {(0, 0): 3, (0, 1): 5, (0, 2): 9, (0, 3): 12, (1, 0): 7, (1, 1): 10, (1, 2): 14}
+    stage_at = {(0, 0): 3, (0, 1): 5, (0, 2): 9, (0, 3): 12, (1, 0): 7, (1, 1): 10, (1, 2): 13}
 
     def ring_move(s, i):
         up_last, down_last = last_up(i), last_down(i)

time: 134 us -> 135 us (level)
  the two profiles are of different devices: /device:TPU:4 before, /device:TPU:16 now
where the time goes in v5:
time: 135 us; the launch traced here: 134 us
  Pallas kernels  131 us (97%)
  other arithmetic  3.08 us (2%)
    pallas_call x1, Pallas kernels, on_device(): pl.pallas_call(functools.partial(kernel, planes, dims), out_shape=(jax.Sh...  131 us
    mul x2, other arithmetic, on_device(): return tuple((total * scale for total in sums))  3.08 us

profile of v5, /device:TPU:16, one launch (start us, length us, event | category | flops | bytes accessed | tf_op | source)
XLA Modules:
  0.0 134.4 jit_solution(8055573922814138418)
XLA Ops:
  0.6 130.6 %shard_map.67 = (f32[192,512]{1,0:T(8,128)}, f32[192,512]{1,0:T(8,128)}, f32[384,512]{1,0:T(8,128)}) custom-call(bf16[192,512]{1,0:T(8,128)(2,1)} %q_in.1, bf16[192,512]{1,0:T(8,128)(2,1)} %p_in.1, bf16[384,512]{1,0:T(8,128)(2,1)} %n_in.1, s32[7,192]{1,0:T(8,128)} %bitcast.1), custom_call_target="tpu_custom_call" | custom-call | tf_op jit(solution)/shard_map/pallas_call | solution.py:748
  131.3 0.0 copy-start
  131.3 2.1 %broadcast_multiply_fusion.1 = (f32[192,512]{1,0:T(8,128)}, f32[192,512]{1,0:T(8,128)}) fusion(f32[192,512]{1,0:T(8,128)} %get-tuple-element.7, f32[192,512]{1,0:T(8,128)} %get-tuple-element.6), kind=kLoop, calls=%fused_computation.1 | loop fusion | flops 196608 | bytes 1572864 | tf_op jit(solution)/shard_map/mul | solution.py:762
  133.4 0.0 copy-done
  133.4 0.9 broadcast_multiply_fusion
Async XLA Ops:
  131.3 2.1 %copy-start = (f32[384,512]{1,0:T(8,128)S(1)}, f32[384,512]{1,0:T(8,128)}, u32[]{:S(2)}) copy-start(f32[384,512]{1,0:T(8,128)} %get-tuple-element.8) | copy-start | bytes 2359300
